TPU v7x, 512 devices: a whole 4x4x16 slice. The times are simulated.
512 devices in a mesh: gx: 16 (over z_lo, core), gy: 32 (over z_hi, y, x).
Axes of the slice: x: 4, y: 4, z: 16 (z_hi: 2, z_lo: 8; z = z_hi * 8 + z_lo), core: 2. Of those that a mesh axis runs over, the one named last changes fastest.
Arguments:
- populations: float32 [19, 256, 512, 128], P(None, 'gx', 'gy'), may hold values from 0 to 1, as said below
- seed_cells: int32 [16, 32, 128], P('gx', 'gy'), may hold values from 0 to 32767
Outputs:
- populations_out: float32 [19, 256, 512, 128], P(None, 'gx', 'gy')
- gradient: float32 [9, 16, 32, 128], P(None, 'gx', 'gy')
- q_value: float32 [16, 32, 128], P('gx', 'gy')
- r_value: float32 [16, 32, 128], P('gx', 'gy')
- vortex_share: float32 [16, 32, 128], P('gx', 'gy')
Inputs may be any that keep to these rules, and one draw needn't show every extreme that they name: `populations`: every population is positive, near its equilibrium for a cell's density and flow.
All inputs are finite; a program needn't handle non-finite values.
Results may differ from a plain program's by a relative error of at most 0.000054.
Values sent between devices are 32-bit elements; how exact they have to be, the bound alone decides.
No kernel may reach another device: no remote copies, remote signals or barrier semaphores. Data moves between devices by JAX's collectives and lax.ppermute only.
A program may use at most 64 MiB of HBM per device.

v0:
```python
import jax
import jax.numpy as jnp
from jax import lax
from jax.sharding import PartitionSpec as P

VELOCITIES = [
    (0, 0, 0),
    (1, 0, 0),
    (-1, 0, 0),
    (0, 1, 0),
    (0, -1, 0),
    (0, 0, 1),
    (0, 0, -1),
    (1, 1, 0),
    (-1, -1, 0),
    (1, -1, 0),
    (-1, 1, 0),
    (1, 0, 1),
    (-1, 0, -1),
    (1, 0, -1),
    (-1, 0, 1),
    (0, 1, 1),
    (0, -1, -1),
    (0, 1, -1),
    (0, -1, 1),
]
WEIGHTS = [1.0 / 3.0] + [1.0 / 18.0] * 6 + [1.0 / 36.0] * 12
RELAX_RATE = 1.6
DIFF_SCALE = 10.0


def padded_2(block, sides, width):
    for axis, dim in sides:
        count = lax.axis_size(axis)
        forward = [(i, i + 1) for i in range(count - 1)]
        forward.append((count - 1, 0))
        backward = [(target, source) for source, target in forward]
        low = lax.ppermute(
            lax.slice_in_dim(block, block.shape[dim] - width, None, axis=dim), axis, forward
        )
        high = lax.ppermute(lax.slice_in_dim(block, 0, width, axis=dim), axis, backward)
        block = jnp.concatenate([low, block, high], axis=dim)
    return block


def velocity(pops):
    density = pops[0]
    for index in range(1, 19):
        density = density + pops[index]
    flows = []
    for axis_number in range(3):
        total = jnp.zeros_like(density)
        for index in range(19):
            weight = VELOCITIES[index][axis_number]
            if weight == 1:
                total = total + pops[index]
            elif weight == -1:
                total = total - pops[index]
        flows.append(total / density)
    return (density, flows)


def collide(pops):
    density, flows = velocity(pops)
    speed_sq = flows[0] * flows[0] + flows[1] * flows[1] + flows[2] * flows[2]
    relaxed = []
    for index in range(19):
        along = (
            VELOCITIES[index][0] * flows[0]
            + VELOCITIES[index][1] * flows[1]
            + VELOCITIES[index][2] * flows[2]
        )
        equil = (
            WEIGHTS[index] * density * (1.0 + 3.0 * along + 4.5 * along * along - 1.5 * speed_sq)
        )
        relaxed.append(pops[index] - RELAX_RATE * (pops[index] - equil))
    return jnp.stack(relaxed)


def shifted(padded_one, index):
    extent_x = padded_one.shape[0] - 2
    extent_y = padded_one.shape[1] - 2
    start_x = 1 - VELOCITIES[index][0]
    start_y = 1 - VELOCITIES[index][1]
    piece = padded_one[start_x : start_x + extent_x, start_y : start_y + extent_y]
    return jnp.roll(piece, VELOCITIES[index][2], axis=2)


def stream_shrink(padded):
    return jnp.stack([shifted(padded[index], index) for index in range(19)])


def invariants(comps):
    q_sum = jnp.zeros_like(comps[0])
    for row in range(3):
        for col in range(3):
            q_sum = q_sum + comps[3 * row + col] * comps[3 * col + row]
    r_sum = jnp.zeros_like(comps[0])
    for row in range(3):
        for col in range(3):
            for third in range(3):
                r_sum = (
                    r_sum + comps[3 * row + col] * comps[3 * col + third] * comps[3 * third + row]
                )
    norm_sq = jnp.zeros_like(comps[0])
    for index in range(9):
        norm_sq = norm_sq + comps[index] * comps[index]
    q_value = -0.5 * q_sum
    r_value = -(1.0 / 3.0) * r_sum
    share = 2.0 * q_value / (norm_sq + 0.25)
    return (q_value, r_value, share)


def per_device(populations, seed_cells):
    current = populations
    for repeat in range(2):
        relaxed = collide(current)
        padded = padded_2(relaxed, (("gx", 1), ("gy", 2)), 1)
        current = stream_shrink(padded)
    density, flows = velocity(current)
    flow_field = jnp.stack(flows)
    rimmed = padded_2(flow_field, (("gx", 1), ("gy", 2)), 1)
    comps = []
    for row in range(3):
        comps.append((rimmed[row, 2:, 1:-1] - rimmed[row, :-2, 1:-1]) * DIFF_SCALE)
        comps.append((rimmed[row, 1:-1, 2:] - rimmed[row, 1:-1, :-2]) * DIFF_SCALE)
        comps.append(
            (jnp.roll(flow_field[row], -1, 2) - jnp.roll(flow_field[row], 1, 2)) * DIFF_SCALE
        )
    tensor = jnp.stack(comps).reshape(9, -1)
    picked = jnp.take(tensor, seed_cells.reshape(-1), axis=1)
    q_value, r_value, share = invariants([picked[index] for index in range(9)])
    count = seed_cells.shape[2]
    return (
        current,
        picked.reshape(9, 1, 1, count),
        q_value.reshape(1, 1, count),
        r_value.reshape(1, 1, count),
        share.reshape(1, 1, count),
    )


def solution(mesh):
    in_specs = (P(None, "gx", "gy", None), P("gx", "gy", None))
    out_specs = (
        P(None, "gx", "gy", None),
        P(None, "gx", "gy", None),
        P("gx", "gy", None),
        P("gx", "gy", None),
        P("gx", "gy", None),
    )
    return jax.shard_map(
        per_device, mesh=mesh, in_specs=in_specs, out_specs=out_specs, check_vma=False
    )
```

profile of v0, /device:TPU:30, one launch (start us, length us, event | category | flops | bytes accessed | tf_op | source)
XLA Modules:
  0.0 179.0 jit_solution(4934183901806503285)
XLA Ops:
  0.6 2.2 %fusion.6 = (f32[19,16,16,128]{3,2,1,0:T(8,128)S(1)}, f32[1,16,16,128]{3,2,1,0:T(8,128)S(1)}, f32[1,16,16,128]{3,2,1,0:T(8,128)S(1)}, f32[1,16,16,128]{3,2,1,0:T...) fusion(f32[19,16,16,128]{3,2,1,0:T(8,128)} %param.2), kind=kLoop, calls=%fused_computation.91 | loop fusion | flops 2293759 | bytes 3276800
  4.7 12.6 %collective-permute-start.1 = (f32[19,1,16,128]{3,2,1,0:T(8,128)S(1)}, f32[19,1,16,128]{3,2,1,0:T(8,128)S(1)}, u32[]{:S(2)}, u32[]{:S(2)}) collective-permute-start(f32[19,1,16,128]{3,2,1,0:T(8,128)S(1)} %get-tuple-element.106), channel_id=1, source_target_pairs={{32,0},{64,32},{96,64},{128,96},{160,128},{192,160},{224,192},{256... | collective-permute-start | bytes 466952 | tf_op jit(solution)/shard_map/ppermute | solution.py:41
  17.3 1.9 %collective-permute-start = (f32[19,1,16,128]{3,2,1,0:T(8,128)S(1)}, f32[19,1,16,128]{3,2,1,0:T(8,128)S(1)}, u32[]{:S(2)}, u32[]{:S(2)}) collective-permute-start(f32[19,1,16,128]{3,2,1,0:T(8,128)S(1)} %get-tuple-element.105), channel_id=1, source_target_pairs={{0,32},{32,64},{64,96},{96,128},{128,160},{160,192},{192,224},{224... | collective-permute-start | bytes 466952 | tf_op jit(solution)/shard_map/ppermute | solution.py:38
  19.2 0.8 collective-permute-done.1
  20.0 10.4 %collective-permute-done = f32[19,1,16,128]{3,2,1,0:T(8,128)S(1)} collective-permute-done((f32[19,1,16,128]{3,2,1,0:T(8,128)S(1)}, f32[19,1,16,128]{3,2,1,0:T(8,128)S(1)}, u32[]{:S(2)}, u32[]{:S(2)}) %collective-permute-start) | collective-permute-done | bytes 155680 | tf_op jit(solution)/shard_map/ppermute | solution.py:38
  30.7 2.7 %collective-permute-start.3 = (f32[19,18,1,128]{3,2,1,0:T(1,128)S(1)}, f32[19,18,1,128]{3,2,1,0:T(1,128)S(1)}, u32[]{:S(2)}, u32[]{:S(2)}) collective-permute-start(f32[19,18,1,128]{3,2,1,0:T(1,128)S(1)} %get-tuple-element.102), channel_id=1, source_target_pairs={{1,0},{2,1},{3,2},{4,3},{5,4},{6,5},{7,6},{8,7},{9,8},{10,9},{11,1... | collective-permute-start | bytes 525320 | tf_op jit(solution)/shard_map/ppermute | solution.py:41
  33.4 16.0 %collective-permute-start.2 = (f32[19,18,1,128]{3,2,1,0:T(1,128)S(1)}, f32[19,18,1,128]{3,2,1,0:T(1,128)S(1)}, u32[]{:S(2)}, u32[]{:S(2)}) collective-permute-start(f32[19,18,1,128]{3,2,1,0:T(1,128)S(1)} %get-tuple-element.101), channel_id=1, source_target_pairs={{0,1},{1,2},{2,3},{3,4},{4,5},{5,6},{6,7},{7,8},{8,9},{9,10},{10,1... | collective-permute-start | bytes 525320 | tf_op jit(solution)/shard_map/ppermute | solution.py:38
  49.5 2.1 %collective-permute-done.3 = f32[19,18,1,128]{3,2,1,0:T(1,128)S(1)} collective-permute-done((f32[19,18,1,128]{3,2,1,0:T(1,128)S(1)}, f32[19,18,1,128]{3,2,1,0:T(1,128)S(1)}, u32[]{:S(2)}, u32[]{:S(2)}) %collective-permute-start.3) | collective-permute-done | bytes 175136 | tf_op jit(solution)/shard_map/ppermute | solution.py:41
  51.6 1.4 collective-permute-done.2
  52.9 0.7 pad_maximum_fusion
  55.1 0.6 fusion.140
  57.5 5.0 %collective-permute-start.5 = (f32[19,1,16,128]{3,2,1,0:T(8,128)S(1)}, f32[19,1,16,128]{3,2,1,0:T(8,128)S(1)}, u32[]{:S(2)}, u32[]{:S(2)}) collective-permute-start(f32[19,1,16,128]{3,2,1,0:T(8,128)S(1)} %get-tuple-element.104), channel_id=1, source_target_pairs={{32,0},{64,32},{96,64},{128,96},{160,128},{192,160},{224,192},{256... | collective-permute-start | bytes 466952 | tf_op jit(solution)/shard_map/ppermute | solution.py:41
  62.5 1.9 %collective-permute-start.4 = (f32[19,1,16,128]{3,2,1,0:T(8,128)S(1)}, f32[19,1,16,128]{3,2,1,0:T(8,128)S(1)}, u32[]{:S(2)}, u32[]{:S(2)}) collective-permute-start(f32[19,1,16,128]{3,2,1,0:T(8,128)S(1)} %get-tuple-element.103), channel_id=1, source_target_pairs={{0,32},{32,64},{64,96},{96,128},{128,160},{160,192},{192,224},{224... | collective-permute-start | bytes 466952 | tf_op jit(solution)/shard_map/ppermute | solution.py:38
  64.5 1.0 collective-permute-done.5
  65.5 10.1 %collective-permute-done.4 = f32[19,1,16,128]{3,2,1,0:T(8,128)S(1)} collective-permute-done((f32[19,1,16,128]{3,2,1,0:T(8,128)S(1)}, f32[19,1,16,128]{3,2,1,0:T(8,128)S(1)}, u32[]{:S(2)}, u32[]{:S(2)}) %collective-permute-start.4) | collective-permute-done | bytes 155680 | tf_op jit(solution)/shard_map/ppermute | solution.py:38
  75.9 1.9 %collective-permute-start.7 = (f32[19,18,1,128]{3,2,1,0:T(1,128)S(1)}, f32[19,18,1,128]{3,2,1,0:T(1,128)S(1)}, u32[]{:S(2)}, u32[]{:S(2)}) collective-permute-start(f32[19,18,1,128]{3,2,1,0:T(1,128)S(1)} %get-tuple-element.100), channel_id=1, source_target_pairs={{1,0},{2,1},{3,2},{4,3},{5,4},{6,5},{7,6},{8,7},{9,8},{10,9},{11,1... | collective-permute-start | bytes 525320 | tf_op jit(solution)/shard_map/ppermute | solution.py:41
  77.9 18.8 %collective-permute-start.6 = (f32[19,18,1,128]{3,2,1,0:T(1,128)S(1)}, f32[19,18,1,128]{3,2,1,0:T(1,128)S(1)}, u32[]{:S(2)}, u32[]{:S(2)}) collective-permute-start(f32[19,18,1,128]{3,2,1,0:T(1,128)S(1)} %get-tuple-element.99), channel_id=1, source_target_pairs={{0,1},{1,2},{2,3},{3,4},{4,5},{5,6},{6,7},{7,8},{8,9},{9,10},{10,1... | collective-permute-start | bytes 525320 | tf_op jit(solution)/shard_map/ppermute | solution.py:38
  96.7 4.3 %collective-permute-done.7 = f32[19,18,1,128]{3,2,1,0:T(1,128)S(1)} collective-permute-done((f32[19,18,1,128]{3,2,1,0:T(1,128)S(1)}, f32[19,18,1,128]{3,2,1,0:T(1,128)S(1)}, u32[]{:S(2)}, u32[]{:S(2)}) %collective-permute-start.7) | collective-permute-done | bytes 175136 | tf_op jit(solution)/shard_map/ppermute | solution.py:41
  101.0 3.5 %collective-permute-done.6 = f32[19,18,1,128]{3,2,1,0:T(1,128)S(1)} collective-permute-done((f32[19,18,1,128]{3,2,1,0:T(1,128)S(1)}, f32[19,18,1,128]{3,2,1,0:T(1,128)S(1)}, u32[]{:S(2)}, u32[]{:S(2)}) %collective-permute-start.6) | collective-permute-done | bytes 175136 | tf_op jit(solution)/shard_map/ppermute | solution.py:38
  104.5 0.7 pad_maximum_fusion.1
  108.6 1.9 %collective-permute-start.9 = (f32[3,1,16,128]{3,2,1,0:T(8,128)S(1)}, f32[3,1,16,128]{3,2,1,0:T(8,128)S(1)}, u32[]{:S(2)}, u32[]{:S(2)}) collective-permute-start(f32[3,1,16,128]{3,2,1,0:T(8,128)S(1)} %get-tuple-element.114), channel_id=1, source_target_pairs={{0,32},{32,64},{64,96},{96,128},{128,160},{160,192},{192,224},{224... | collective-permute-start | bytes 73736 | tf_op jit(solution)/shard_map/ppermute | solution.py:38
  110.5 10.2 %collective-permute-start.8 = (f32[3,1,16,128]{3,2,1,0:T(8,128)S(1)}, f32[3,1,16,128]{3,2,1,0:T(8,128)S(1)}, u32[]{:S(2)}, u32[]{:S(2)}) collective-permute-start(f32[3,1,16,128]{3,2,1,0:T(8,128)S(1)} %get-tuple-element.113), channel_id=1, source_target_pairs={{32,0},{64,32},{96,64},{128,96},{160,128},{192,160},{224,192},{256... | collective-permute-start | bytes 73736 | tf_op jit(solution)/shard_map/ppermute | solution.py:41
  121.2 1.1 collective-permute-done.8
  122.3 17.3 %collective-permute-start.11 = (f32[3,18,1,128]{3,2,1,0:T(1,128)S(1)}, f32[3,18,1,128]{3,2,1,0:T(1,128)S(1)}, u32[]{:S(2)}, u32[]{:S(2)}) collective-permute-start(f32[3,18,1,128]{3,2,1,0:T(1,128)S(1)} %get-tuple-element.112), channel_id=1, source_target_pairs={{0,1},{1,2},{2,3},{3,4},{4,5},{5,6},{6,7},{7,8},{8,9},{9,10},{10,1... | collective-permute-start | bytes 82952 | tf_op jit(solution)/shard_map/ppermute | solution.py:38
  139.6 1.9 %collective-permute-start.10 = (f32[3,18,1,128]{3,2,1,0:T(1,128)S(1)}, f32[3,18,1,128]{3,2,1,0:T(1,128)S(1)}, u32[]{:S(2)}, u32[]{:S(2)}) collective-permute-start(f32[3,18,1,128]{3,2,1,0:T(1,128)S(1)} %get-tuple-element.111), channel_id=1, source_target_pairs={{1,0},{2,1},{3,2},{4,3},{5,4},{6,5},{7,6},{8,7},{9,8},{10,9},{11,1... | collective-permute-start | bytes 82952 | tf_op jit(solution)/shard_map/ppermute | solution.py:41
  141.5 0.7 fusion.288
  142.2 0.7 fusion.290
  142.9 15.4 %collective-permute-done.10 = f32[3,18,1,128]{3,2,1,0:T(1,128)S(1)} collective-permute-done((f32[3,18,1,128]{3,2,1,0:T(1,128)S(1)}, f32[3,18,1,128]{3,2,1,0:T(1,128)S(1)}, u32[]{:S(2)}, u32[]{:S(2)}) %collective-permute-start.10) | collective-permute-done | bytes 27680 | tf_op jit(solution)/shard_map/ppermute | solution.py:41
  158.5 3.0 %stack.229 = f32[9,32768]{1,0:T(8,128)S(1)} concatenate(f32[1,32768]{1,0:T(1,128)} %bitcast.586, f32[1,32768]{1,0:T(1,128)S(1)} %bitcast.582, f32[1,32768]{1,0:T(1,128)S(1)} %bitcast.579, f32[1,32768]{1,0:T(1,128)} %bitcast.587, f32[1,32768]{1,0:T(1,128)S(1)} %bitcast.583, f32[1,32768]{1,0:T(1,128)S(1)} %bitcast.580, f32[1,32768]{1,0:T(1,128)S(1)} %bitcast.585, ...), dimensions={0} | concatenate | bytes 2359296 | tf_op jit(solution)/shard_map/stack | solution.py:130
  161.4 8.8 %copy.36 = f32[9,32768]{0,1:T(8,128)} copy(f32[9,32768]{1,0:T(8,128)S(1)} %stack.229) | data formatting | bytes 2359296 | tf_op jit(solution)/shard_map/stack | solution.py:130
  170.3 6.4 %gather_fusion = f32[128,9]{1,0:T(8,128)S(1)} fusion(f32[9,32768]{0,1:T(8,128)} %copy.36, s32[1024]{0:T(1024)S(1)} %pad_clamp_fusion), kind=kCustom, calls=%fused_computation | custom fusion | bytes 9728 | tf_op jit(solution)/shard_map/jit(_take)/gather | solution.py:131
  176.9 0.7 copy.37
  (131 shorter events, 10.5 us)
Async XLA Ops:
  0.6 2.5 %copy-start = (f32[19,16,16,128]{3,2,1,0:T(8,128)S(1)}, f32[19,16,16,128]{3,2,1,0:T(8,128)}, u32[]{:S(2)}) copy-start(f32[19,16,16,128]{3,2,1,0:T(8,128)} %param.2) | copy-start | bytes 7471108
  4.7 15.3 %collective-permute-start.1 = (f32[19,1,16,128]{3,2,1,0:T(8,128)S(1)}, f32[19,1,16,128]{3,2,1,0:T(8,128)S(1)}, u32[]{:S(2)}, u32[]{:S(2)}) collective-permute-start(f32[19,1,16,128]{3,2,1,0:T(8,128)S(1)} %get-tuple-element.106), channel_id=1, source_target_pairs={{32,0},{64,32},{96,64},{128,96},{160,128},{192,160},{224,192},{256... | collective-permute-start | bytes 466952 | tf_op jit(solution)/shard_map/ppermute | solution.py:41
  17.3 13.2 %collective-permute-start = (f32[19,1,16,128]{3,2,1,0:T(8,128)S(1)}, f32[19,1,16,128]{3,2,1,0:T(8,128)S(1)}, u32[]{:S(2)}, u32[]{:S(2)}) collective-permute-start(f32[19,1,16,128]{3,2,1,0:T(8,128)S(1)} %get-tuple-element.105), channel_id=1, source_target_pairs={{0,32},{32,64},{64,96},{96,128},{128,160},{160,192},{192,224},{224... | collective-permute-start | bytes 466952 | tf_op jit(solution)/shard_map/ppermute | solution.py:38
  30.7 20.9 %collective-permute-start.3 = (f32[19,18,1,128]{3,2,1,0:T(1,128)S(1)}, f32[19,18,1,128]{3,2,1,0:T(1,128)S(1)}, u32[]{:S(2)}, u32[]{:S(2)}) collective-permute-start(f32[19,18,1,128]{3,2,1,0:T(1,128)S(1)} %get-tuple-element.102), channel_id=1, source_target_pairs={{1,0},{2,1},{3,2},{4,3},{5,4},{6,5},{7,6},{8,7},{9,8},{10,9},{11,1... | collective-permute-start | bytes 525320 | tf_op jit(solution)/shard_map/ppermute | solution.py:41
  33.4 19.5 %collective-permute-start.2 = (f32[19,18,1,128]{3,2,1,0:T(1,128)S(1)}, f32[19,18,1,128]{3,2,1,0:T(1,128)S(1)}, u32[]{:S(2)}, u32[]{:S(2)}) collective-permute-start(f32[19,18,1,128]{3,2,1,0:T(1,128)S(1)} %get-tuple-element.101), channel_id=1, source_target_pairs={{0,1},{1,2},{2,3},{3,4},{4,5},{5,6},{6,7},{7,8},{8,9},{9,10},{10,1... | collective-permute-start | bytes 525320 | tf_op jit(solution)/shard_map/ppermute | solution.py:38
  57.0 7.5 %copy-start.2 = (s32[1,1,128]{2,1,0:T(1,128)S(1)}, s32[1,1,128]{2,1,0:T(1,128)}, u32[]{:S(2)}) copy-start(s32[1,1,128]{2,1,0:T(1,128)} %param.3) | copy-start | bytes 1540
  57.5 8.1 %collective-permute-start.5 = (f32[19,1,16,128]{3,2,1,0:T(8,128)S(1)}, f32[19,1,16,128]{3,2,1,0:T(8,128)S(1)}, u32[]{:S(2)}, u32[]{:S(2)}) collective-permute-start(f32[19,1,16,128]{3,2,1,0:T(8,128)S(1)} %get-tuple-element.104), channel_id=1, source_target_pairs={{32,0},{64,32},{96,64},{128,96},{160,128},{192,160},{224,192},{256... | collective-permute-start | bytes 466952 | tf_op jit(solution)/shard_map/ppermute | solution.py:41
  62.5 13.2 %collective-permute-start.4 = (f32[19,1,16,128]{3,2,1,0:T(8,128)S(1)}, f32[19,1,16,128]{3,2,1,0:T(8,128)S(1)}, u32[]{:S(2)}, u32[]{:S(2)}) collective-permute-start(f32[19,1,16,128]{3,2,1,0:T(8,128)S(1)} %get-tuple-element.103), channel_id=1, source_target_pairs={{0,32},{32,64},{64,96},{96,128},{128,160},{160,192},{192,224},{224... | collective-permute-start | bytes 466952 | tf_op jit(solution)/shard_map/ppermute | solution.py:38
  75.9 25.1 %collective-permute-start.7 = (f32[19,18,1,128]{3,2,1,0:T(1,128)S(1)}, f32[19,18,1,128]{3,2,1,0:T(1,128)S(1)}, u32[]{:S(2)}, u32[]{:S(2)}) collective-permute-start(f32[19,18,1,128]{3,2,1,0:T(1,128)S(1)} %get-tuple-element.100), channel_id=1, source_target_pairs={{1,0},{2,1},{3,2},{4,3},{5,4},{6,5},{7,6},{8,7},{9,8},{10,9},{11,1... | collective-permute-start | bytes 525320 | tf_op jit(solution)/shard_map/ppermute | solution.py:41
  77.9 26.7 %collective-permute-start.6 = (f32[19,18,1,128]{3,2,1,0:T(1,128)S(1)}, f32[19,18,1,128]{3,2,1,0:T(1,128)S(1)}, u32[]{:S(2)}, u32[]{:S(2)}) collective-permute-start(f32[19,18,1,128]{3,2,1,0:T(1,128)S(1)} %get-tuple-element.99), channel_id=1, source_target_pairs={{0,1},{1,2},{2,3},{3,4},{4,5},{5,6},{6,7},{7,8},{8,9},{9,10},{10,1... | collective-permute-start | bytes 525320 | tf_op jit(solution)/shard_map/ppermute | solution.py:38
  108.5 49.9 %copy-start.1 = (f32[19,16,16,128]{3,2,1,0:T(8,128)}, f32[19,16,16,128]{3,2,1,0:T(8,128)S(1)}, u32[]{:S(2)}) copy-start(f32[19,16,16,128]{3,2,1,0:T(8,128)S(1)} %bitcast_dynamic-update-slice_fusion) | copy-start | bytes 7471108
  108.6 12.6 %collective-permute-start.9 = (f32[3,1,16,128]{3,2,1,0:T(8,128)S(1)}, f32[3,1,16,128]{3,2,1,0:T(8,128)S(1)}, u32[]{:S(2)}, u32[]{:S(2)}) collective-permute-start(f32[3,1,16,128]{3,2,1,0:T(8,128)S(1)} %get-tuple-element.114), channel_id=1, source_target_pairs={{0,32},{32,64},{64,96},{96,128},{128,160},{160,192},{192,224},{224... | collective-permute-start | bytes 73736 | tf_op jit(solution)/shard_map/ppermute | solution.py:38
  110.5 11.8 %collective-permute-start.8 = (f32[3,1,16,128]{3,2,1,0:T(8,128)S(1)}, f32[3,1,16,128]{3,2,1,0:T(8,128)S(1)}, u32[]{:S(2)}, u32[]{:S(2)}) collective-permute-start(f32[3,1,16,128]{3,2,1,0:T(8,128)S(1)} %get-tuple-element.113), channel_id=1, source_target_pairs={{32,0},{64,32},{96,64},{128,96},{160,128},{192,160},{224,192},{256... | collective-permute-start | bytes 73736 | tf_op jit(solution)/shard_map/ppermute | solution.py:41
  122.3 20.6 %collective-permute-start.11 = (f32[3,18,1,128]{3,2,1,0:T(1,128)S(1)}, f32[3,18,1,128]{3,2,1,0:T(1,128)S(1)}, u32[]{:S(2)}, u32[]{:S(2)}) collective-permute-start(f32[3,18,1,128]{3,2,1,0:T(1,128)S(1)} %get-tuple-element.112), channel_id=1, source_target_pairs={{0,1},{1,2},{2,3},{3,4},{4,5},{5,6},{6,7},{7,8},{8,9},{9,10},{10,1... | collective-permute-start | bytes 82952 | tf_op jit(solution)/shard_map/ppermute | solution.py:38
  139.6 18.7 %collective-permute-start.10 = (f32[3,18,1,128]{3,2,1,0:T(1,128)S(1)}, f32[3,18,1,128]{3,2,1,0:T(1,128)S(1)}, u32[]{:S(2)}, u32[]{:S(2)}) collective-permute-start(f32[3,18,1,128]{3,2,1,0:T(1,128)S(1)} %get-tuple-element.111), channel_id=1, source_target_pairs={{1,0},{2,1},{3,2},{4,3},{5,4},{6,5},{7,6},{8,7},{9,8},{10,9},{11,1... | collective-permute-start | bytes 82952 | tf_op jit(solution)/shard_map/ppermute | solution.py:41
where the time goes:
time: 180 us; the launch traced here: 179 us
  starting transfers between devices  92.4 us (51%)
  waiting for transfers between devices  50.2 us (28%)
  local copies, waits for them, and re-layouts  23.1 us (13%)
  other arithmetic  11.7 us (6%)
    ppermute x6, starting transfers between devices, padded_2(): lax.ppermute(lax.slice_in_dim(block, block.shape[dim] - width, None, axis...  57.9 us
    ppermute x6, starting transfers between devices, padded_2(): lax.ppermute(lax.slice_in_dim(block, 0, width, axis=dim), axis, backward)  34.5 us
    ppermute x6, waiting for transfers between devices, padded_2(): lax.ppermute(lax.slice_in_dim(block, block.shape[dim] - width, None, axis...  25.4 us
    ppermute x6, waiting for transfers between devices, padded_2(): lax.ppermute(lax.slice_in_dim(block, 0, width, axis=dim), axis, backward)  24.7 us
    another operation x2, local copies, waits for them, and re-layouts, per_device(): tensor = jnp.stack(comps).reshape(9, -1)  11.8 us
    gather x1, local copies, waits for them, and re-layouts, per_device(): picked = jnp.take(tensor, seed_cells.reshape(-1), axis=1)  6.41 us
    unnamed x38, other arithmetic  5.81 us
  transfers between devices with their start and end apart: 12, of which 10 were waited for; matrix products, arithmetic and copies ran while one was open for 1% of the time, Pallas kernels for 0%

commit v1 on v0

v1 whole, which is shorter than its diff:
```python
import jax
import jax.numpy as jnp
from jax import lax
from jax.experimental import pallas as pl
from jax.experimental.pallas import tpu as pltpu
from jax.sharding import PartitionSpec as P

C = [
    (0, 0, 0),
    (1, 0, 0),
    (-1, 0, 0),
    (0, 1, 0),
    (0, -1, 0),
    (0, 0, 1),
    (0, 0, -1),
    (1, 1, 0),
    (-1, -1, 0),
    (1, -1, 0),
    (-1, 1, 0),
    (1, 0, 1),
    (-1, 0, -1),
    (1, 0, -1),
    (-1, 0, 1),
    (0, 1, 1),
    (0, -1, -1),
    (0, 1, -1),
    (0, -1, 1),
]
W = [1.0 / 3.0] + [1.0 / 18.0] * 6 + [1.0 / 36.0] * 12
RATE = 1.6
KEEP = 1.0 - RATE
SCALE = 10.0
ALL = list(range(19))
PAIRS = [(1, 2), (3, 4), (5, 6), (7, 8), (9, 10), (11, 12), (13, 14), (15, 16), (17, 18)]
N = 16
NZ = 128
SEEDS = 128
F32 = jnp.float32
BF16 = jnp.bfloat16
ROWS = {0: (0, 1, 2), 1: (15, 14, 13)}
OWN_ROWS = (0, 1, 2, 13, 14, 15)
T_AT = 10
T_LEN = 40
WIDE = 24
YW = 20
N_A = 5
S_OFF = 13 * YW
Y_LEN = S_OFF + 4 * N
PAD_LEN = 336
V_ROWS = (-1, 0, 1, 14, 15, 16)
VMEM_LIMIT = 48 * 1024 * 1024


def x_fields(direction):
    out = [(0, i) for i in ALL]
    out += [(1, i) for i in ALL if C[i][0] != -direction]
    out += [(2, i) for i in ALL if C[i][0] == direction]
    return out


X_POS = {d: {key: k for k, key in enumerate(x_fields(d))} for d in (-1, 1)}
X_LEN = len(X_POS[1])


def zroll(v, shift):
    shift = shift % NZ
    return pltpu.roll(v, shift, axis=v.ndim - 1) if shift else v


def add_up(terms):
    terms = list(terms)
    while len(terms) > 1:
        terms = [a + b for a, b in zip(terms[::2], terms[1::2])] + (
            [terms[-1]] if len(terms) % 2 else []
        )
    return terms[0]


def moment(f, axis, indices=ALL):
    plus = [f[i] for i in indices if C[i][axis] == 1]
    minus = [f[i] for i in indices if C[i][axis] == -1]
    if plus and minus:
        return add_up(plus) - add_up(minus)
    if plus:
        return add_up(plus)
    return -add_up(minus)


def moments(f, indices=ALL):
    return [add_up(f[i] for i in indices)] + [moment(f, axis, indices) for axis in range(3)]


def equil(mom, wanted):
    rho = mom[0]
    inv = 1.0 / rho
    u = [m * inv for m in mom[1:]]
    base = 1.0 - 1.5 * (u[0] * u[0] + u[1] * u[1] + u[2] * u[2])
    r18 = rho * (RATE / 18.0)
    r36 = rho * (RATE / 36.0)
    out = {}
    if 0 in wanted:
        out[0] = rho * (RATE / 3.0) * base
    for a, b in PAIRS:
        if a not in wanted and b not in wanted:
            continue
        along = None
        for axis in range(3):
            c = C[a][axis]
            if c:
                term = u[axis] if c == 1 else -u[axis]
                along = term if along is None else along + term
        r = r18 if a < 7 else r36
        even = r * (base + 4.5 * along * along)
        odd = r * (3.0 * along)
        if a in wanted:
            out[a] = even + odd
        if b in wanted:
            out[b] = even - odd
    return out


def collide(f, wanted=ALL):
    eq = equil(moments(f), wanted)
    return {i: KEEP * f[i] + eq[i] for i in wanted}


def side_parts(s):
    toward = [i for i in ALL if C[i][1] == s]
    par = [i for i in ALL if C[i][1] == 0]
    away = [i for i in ALL if C[i][1] == -s]
    return toward, par, away


def x_pack_kernel(f_hbm, a_out, b_out, buf, sems):
    copies = [
        pltpu.make_async_copy(f_hbm.at[:, pl.ds(start, 3)], buf.at[side], sems.at[side])
        for side, start in ((0, 0), (1, N - 3))
    ]
    for copy in copies:
        copy.start()
    even = lax.rem(lax.axis_index("gx"), 2) == 0
    for side, direction in ((0, -1), (1, 1)):
        copies[side].wait()
        for layer in range(3):
            at = layer if side == 0 else 2 - layer
            wanted = [i for i in ALL if (layer, i) in X_POS[direction]]
            g = collide([buf[side, i, at] for i in ALL], wanted)

            def put(out, layer=layer, g=g, direction=direction):
                for i, value in g.items():
                    out[X_POS[direction][(layer, i)]] = value

            first = even if side == 1 else jnp.logical_not(even)
            pl.when(first)(lambda put=put: put(a_out))
            pl.when(jnp.logical_not(first))(lambda put=put: put(b_out))


def rows_kernel(f_ref, g_out):
    for r, y in enumerate(OWN_ROWS):
        g = collide([f_ref[i, pl.ds(y, N, stride=N), :] for i in ALL])
        for i in ALL:
            g_out[r, i] = g[i]


def y_pack_kernel(g_ref, xa, xb, a_out, b_out, lo, hi, t, hs):
    even_x = lax.rem(lax.axis_index("gx"), 2) == 0
    even_y = lax.rem(lax.axis_index("gy"), 2) == 0

    @pl.when(even_x)
    def _():
        hi[...] = xa[...]
        lo[...] = xb[...]

    @pl.when(jnp.logical_not(even_x))
    def _():
        hi[...] = xb[...]
        lo[...] = xa[...]

    for r, y in enumerate(OWN_ROWS):
        for i in ALL:
            t[r, i, pl.ds(T_AT, N)] = g_ref[r, i]
        for layer, i in x_fields(-1):
            t[r, i, pl.ds(T_AT + N + layer, 1)] = hi[X_POS[-1][(layer, i)], pl.ds(y, 1)]
        for layer, i in x_fields(1):
            t[r, i, pl.ds(T_AT - 1 - layer, 1)] = lo[X_POS[1][(layer, i)], pl.ds(y, 1)]

    for side, s in ((0, -1), (1, 1)):
        rows = [OWN_ROWS.index(y) for y in ROWS[side]]
        toward, par, away = side_parts(s)

        def moved(r, i, at=T_AT - 2, length=WIDE, steps=1):
            return zroll(t[r, i, pl.ds(at - steps * C[i][0], length)], steps * C[i][2])

        first = [moved(rows[0], i) for i in toward]
        beyond = {i: moved(rows[1], i) for i in toward}
        beside = {i: moved(rows[0], i) for i in par}
        both = {**beyond, **beside}
        mom = moments(both, toward + par)
        full = {i: moved(rows[0], i) for i in away}
        full.update({i: moved(rows[1], i) for i in par})
        full.update({i: moved(rows[2], i) for i in toward})
        relaxed = collide(full, toward)
        for k, i in enumerate(toward):
            hs[side, k, pl.ds(8, WIDE)] = relaxed[i]
        arrive = {
            i: zroll(hs[side, k, pl.ds(T_AT - C[i][0], N)], C[i][2]) for k, i in enumerate(toward)
        }
        for i in par:
            arrive[i] = KEEP * moved(rows[0], i, T_AT, N, 2)
        sums = moments(arrive, toward + par)
        parts = [(k * YW, v[:YW]) for k, v in enumerate(first)]
        parts += [((N_A + k) * YW, beyond[i][:YW]) for k, i in enumerate(toward)]
        parts += [((2 * N_A + k) * YW, v[:YW]) for k, v in enumerate((mom[0], mom[1], mom[3]))]
        parts += [(S_OFF + k * N, v) for k, v in enumerate(sums)]

        def put(out, parts=parts):
            for at, value in parts:
                out[pl.ds(at, value.shape[0])] = value

        to_a = even_y if side == 1 else jnp.logical_not(even_y)
        pl.when(to_a)(lambda put=put: put(a_out))
        pl.when(jnp.logical_not(to_a))(lambda put=put: put(b_out))


def seed_parts(seeds):
    zs = lax.rem(seeds, NZ)
    ys = lax.rem(lax.div(seeds, NZ), N)
    xs = lax.div(seeds, NZ * N)
    return xs, ys, zs


def one_hots(rx, ry, xs, ys):
    along_x = jnp.where(
        ry == ys, jnp.where(rx == xs + 1, 1.0, 0.0) - jnp.where(rx == xs - 1, 1.0, 0.0), 0.0
    )
    along_y = jnp.where(
        rx == xs, jnp.where(ry == ys + 1, 1.0, 0.0) - jnp.where(ry == ys - 1, 1.0, 0.0), 0.0
    )
    here = jnp.where((rx == xs) & (ry == ys), 1.0, 0.0)
    return jnp.concatenate([along_x, along_y, here], axis=1).astype(BF16)


def split3(v):
    hi = v.astype(BF16)
    rest = v - hi.astype(F32)
    mid = rest.astype(BF16)
    low = (rest - mid.astype(F32)).astype(BF16)
    return hi, mid, low


def picks(v, hots, zs):
    iz = lax.broadcasted_iota(jnp.int32, (NZ, SEEDS), 0)
    here = jnp.where(iz == zs, 1.0, 0.0)
    up = jnp.where(iz == lax.rem(zs + 1, NZ), 1.0, 0.0)
    down = jnp.where(iz == lax.rem(zs + NZ - 1, NZ), 1.0, 0.0)
    across = up - down
    out = []
    for comp in range(3):
        total = None
        for part in split3(v[comp]):
            got = lax.dot_general(
                part, hots, (((0,), (0,)), ((), ())), preferred_element_type=F32
            )
            total = got if total is None else total + got
        for kind in range(3):
            mask = across if kind == 2 else here
            piece = total[:, kind * SEEDS : (kind + 1) * SEEDS]
            out.append(jnp.sum(piece * mask, axis=0, keepdims=True))
    return out


def inside_kernel(f_ref, g_ref, xa, xb, seed_ref, f_out, fw_out, qw_out, pm_out, pick_out, hot_out, g, h, t, m, v):
    even_x = lax.rem(lax.axis_index("gx"), 2) == 0

    def halo(x_hi, x_lo):
        for layer, i in x_fields(-1):
            g[i, 3 + N + layer] = x_hi[X_POS[-1][(layer, i)]]
        for layer, i in x_fields(1):
            g[i, 2 - layer] = x_lo[X_POS[1][(layer, i)]]

    pl.when(even_x)(lambda: halo(xa, xb))
    pl.when(jnp.logical_not(even_x))(lambda: halo(xb, xa))

    def first(x, _):
        out = collide([f_ref[i, x] for i in ALL])
        for i in ALL:
            g[i, x + 3] = out[i]
        return 0

    lax.fori_loop(0, N, first, 0)
    inner = lax.broadcasted_iota(jnp.int32, (N, NZ), 0)
    inner = (inner >= 1) & (inner <= N - 2)

    def shift(value, i):
        if C[i][1]:
            value = pltpu.roll(value, C[i][1] % N, axis=0)
        return zroll(value, C[i][2])

    def second(x, _):
        f = [shift(g[i, x + 1 - C[i][0]], i) for i in ALL]
        out = collide(f)
        for i in ALL:
            h[i, x] = jnp.where(inner, out[i], 0.0)
        return 0

    lax.fori_loop(0, N + 4, second, 0)
    iy = lax.broadcasted_iota(jnp.int32, (N, NZ), 0)
    whole = (iy >= 2) & (iy <= N - 3)

    def third(x, _):
        got = [shift(h[i, x + 1 - C[i][0]], i) for i in ALL]

        @pl.when((x >= 1) & (x <= N))
        def _():
            for i in ALL:
                f_out[i, x - 1] = got[i]

        mom = moments(got)
        for k in range(4):
            m[k, pl.ds(x * N, N)] = mom[k]
        for k in range(3):
            v[k, pl.ds(x * N, N)] = jnp.where(whole, mom[k + 1] / mom[0], 0.0)
        return 0

    lax.fori_loop(0, N + 2, third, 0)
    pm_out[...] = jnp.ones_like(pm_out)
    for r, y in enumerate((0, 1, 14, 15)):
        for k in range(4):
            pm_out[r, k, pl.ds(1, N + 2)] = m[k, pl.ds(y, N + 2, stride=N), :]

    t[...] = jnp.ones_like(t)
    for r, y in enumerate(OWN_ROWS):
        if y in (2, 13):
            continue
        for i in ALL:
            t[r, i, pl.ds(T_AT, N)] = g_ref[r, i]
            for at in (-3, -2, -1, N, N + 1, N + 2):
                t[r, i, pl.ds(T_AT + at, 1)] = g[i, at + 3, pl.ds(y, 1)]
    for side, s in ((0, 1), (1, -1)):
        rows = [OWN_ROWS.index(y) for y in ROWS[side]]
        toward, par, away = side_parts(s)
        k = 0
        for r, group in ((rows[0], par), (rows[1], away)):
            for i in group:
                fw_out[side, k] = zroll(t[r, i, pl.ds(T_AT - 2 - C[i][0], WIDE)], C[i][2])
                k += 1
        leave = {
            i: zroll(t[rows[0], i, pl.ds(T_AT - 2 - C[i][0], WIDE)], C[i][2]) for i in away
        }
        for k, value in enumerate(moments(leave, away)):
            qw_out[side, k] = value

    xs, ys, zs = seed_parts(seed_ref[...])
    row = lax.broadcasted_iota(jnp.int32, ((N + 2) * N, 1), 0)
    hots = one_hots(lax.div(row, N) - 1, lax.rem(row, N), xs, ys)
    got = picks([v[k] for k in range(3)], hots, zs)
    for k in range(9):
        pick_out[pl.ds(k, 1)] = got[k]
    row = lax.broadcasted_iota(jnp.int32, (6 * WIDE, 1), 0)
    block = lax.div(row, WIDE)
    ry = jnp.where(block < 3, block - 1, block + 11)
    hot_out[...] = one_hots(lax.rem(row, WIDE) - 2, ry, xs, ys)


def outside_kernel(
    ya, yb, f_hbm, fw, qw, pm, pick, hot, seed_ref, out_hbm, grad_out, q_out, r_out, s_out, msg, hs, hp, ep, fs, sems
):
    fetch = pltpu.make_async_copy(f_hbm, fs, sems.at[0])
    fetch.start()
    even_y = lax.rem(lax.axis_index("gy"), 2) == 0

    @pl.when(even_y)
    def _():
        msg[1, pl.ds(0, Y_LEN)] = ya[...]
        msg[0, pl.ds(0, Y_LEN)] = yb[...]

    @pl.when(jnp.logical_not(even_y))
    def _():
        msg[1, pl.ds(0, Y_LEN)] = yb[...]
        msg[0, pl.ds(0, Y_LEN)] = ya[...]

    row_x = lax.broadcasted_iota(jnp.int32, (WIDE, NZ), 0) - 2
    near = (row_x >= -1) & (row_x <= N)
    own = (row_x >= 0) & (row_x < N)
    vel = {}
    patches = []
    for side, s in ((0, 1), (1, -1)):
        toward, par, away = side_parts(s)
        end, before = (0, 1) if side == 0 else (N - 1, N - 2)

        def field(k):
            return msg[side, pl.ds(k * YW, WIDE)]

        f = {i: field(k) for k, i in enumerate(toward)}
        f.update({i: fw[side, k] for k, i in enumerate(par + away)})
        out = collide(f)
        for i in ALL:
            hs[side, i, pl.ds(8, WIDE)] = out[i]
        coming = {i: field(N_A + k) for k, i in enumerate(toward)}
        mom = [
            field(2 * N_A) + qw[side, 0],
            field(2 * N_A + 1) + qw[side, 1],
            moment(coming, 1, toward) + qw[side, 2],
            field(2 * N_A + 2) + qw[side, 3],
        ]
        eq = equil(mom, toward + par)
        for k, i in enumerate(toward):
            hp[side, k, pl.ds(8, WIDE)] = KEEP * coming[i] + eq[i]
        for k, i in enumerate(par):
            ep[side, k, pl.ds(8, WIDE)] = eq[i]

        def moved(ref, k, i):
            return zroll(ref[side, k, pl.ds(8 - C[i][0], WIDE)], C[i][2])

        last = {i: moved(hp, k, i) for k, i in enumerate(toward)}
        last.update({i: moved(hs, i, i) for i in par})
        second = {i: moved(hs, i, i) for i in toward}
        for i in toward + par:
            patches.append((i, end, last[i]))
        for i in toward:
            patches.append((i, before, second[i]))
        beyond = {i: moved(hs, i, i) for i in away}
        beyond.update({i: moved(ep, k, i) for k, i in enumerate(par)})

        for y, base, terms, group, ok in (
            (end, [pm[(3 if side else 0), k] for k in range(4)], last, toward + par, near),
            (before, [pm[(2 if side else 1), k] for k in range(4)], second, toward, near),
            (
                end - s,
                [msg[side, pl.ds(S_OFF + N * k - 2, WIDE)] for k in range(4)],
                beyond,
                away + par,
                own,
            ),
        ):
            total = [a + b for a, b in zip(base, moments(terms, group))]
            inv = 1.0 / total[0]
            vel[y] = [jnp.where(ok, total[k + 1] * inv, 0.0) for k in range(3)]

    fetch.wait()
    for i, y, value in patches:
        fs[i, pl.ds(y, N, stride=N), :] = value[2 : 2 + N]
    store = pltpu.make_async_copy(fs, out_hbm, sems.at[1])
    store.start()
    zs = lax.rem(seed_ref[...], NZ)
    got = picks([jnp.concatenate([vel[y][k] for y in V_ROWS], axis=0) for k in range(3)], hot[...], zs)
    comps = [(got[k] + pick[pl.ds(k, 1)]) * SCALE for k in range(9)]
    q_sum = add_up(comps[3 * a + b] * comps[3 * b + a] for a in range(3) for b in range(3))
    r_sum = add_up(
        comps[3 * a + b] * comps[3 * b + c] * comps[3 * c + a]
        for a in range(3)
        for b in range(3)
        for c in range(3)
    )
    norm = add_up(c * c for c in comps)
    q = -0.5 * q_sum
    for k in range(9):
        grad_out[k, 0] = comps[k]
    q_out[0] = q
    r_out[0] = -(1.0 / 3.0) * r_sum
    s_out[0] = 2.0 * q / (norm + 0.25)
    store.wait()


def swaps(count):
    first = [(i, i ^ 1) for i in range(count)]
    second = []
    for i in range(1, count, 2):
        j = (i + 1) % count
        second += [(i, j), (j, i)]
    return first, second


def shape(*dims):
    return jax.ShapeDtypeStruct(dims, F32)


VM = pl.BlockSpec(memory_space=pltpu.VMEM)
ANY = pl.BlockSpec(memory_space=pl.ANY)


def params():
    return pltpu.CompilerParams(vmem_limit_bytes=VMEM_LIMIT)


def cost(flops, moved):
    return pl.CostEstimate(flops=flops, bytes_accessed=moved, transcendentals=0)


def per_device(populations, seed_cells):
    dma = pltpu.SemaphoreType.DMA
    vmem = pltpu.VMEM
    x_first, x_second = swaps(lax.axis_size("gx"))
    y_first, y_second = swaps(lax.axis_size("gy"))
    flat = populations.reshape(19, N * N, NZ)
    seeds = seed_cells.reshape(1, SEEDS)

    xa, xb = pl.pallas_call(
        x_pack_kernel,
        out_shape=[shape(X_LEN, N, NZ)] * 2,
        in_specs=[ANY],
        out_specs=[VM] * 2,
        scratch_shapes=[vmem((2, 19, 3, N, NZ), F32), dma((2,))],
        compiler_params=params(),
        cost_estimate=cost(5_000_000, 1_500_000),
        name="x_pack",
    )(populations)
    xb = lax.ppermute(xb, "gx", x_second)
    xa = lax.ppermute(xa, "gx", x_first)
    g_rows = pl.pallas_call(
        rows_kernel,
        out_shape=shape(6, 19, N, NZ),
        in_specs=[VM],
        out_specs=VM,
        compiler_params=params(),
        cost_estimate=cost(5_000_000, 3_500_000),
        name="end_rows",
    )(flat)
    ya, yb = pl.pallas_call(
        y_pack_kernel,
        out_shape=[shape(Y_LEN, NZ)] * 2,
        in_specs=[VM] * 3,
        out_specs=[VM] * 2,
        scratch_shapes=[
            vmem((X_LEN, N, NZ), F32),
            vmem((X_LEN, N, NZ), F32),
            vmem((6, 19, T_LEN, NZ), F32),
            vmem((2, N_A, T_LEN, NZ), F32),
        ],
        compiler_params=params(),
        cost_estimate=cost(5_000_000, 2_000_000),
        name="y_pack",
    )(g_rows, xa, xb)
    yb = lax.ppermute(yb, "gy", y_second)
    ya = lax.ppermute(ya, "gy", y_first)
    inside, fw, qw, pm, pick, hot = pl.pallas_call(
        inside_kernel,
        out_shape=[
            shape(19, N, N, NZ),
            shape(2, 14, WIDE, NZ),
            shape(2, 4, WIDE, NZ),
            shape(4, 4, WIDE, NZ),
            shape(9, SEEDS),
            jax.ShapeDtypeStruct((6 * WIDE, 3 * SEEDS), BF16),
        ],
        in_specs=[VM] * 5,
        out_specs=[VM] * 6,
        scratch_shapes=[
            vmem((19, N + 6, N, NZ), F32),
            vmem((19, N + 4, N, NZ), F32),
            vmem((6, 19, T_LEN, NZ), F32),
            vmem((4, (N + 2) * N, NZ), F32),
            vmem((3, (N + 2) * N, NZ), F32),
        ],
        compiler_params=params(),
        cost_estimate=cost(50_000_000, 30_000_000),
        name="inside",
    )(populations, g_rows, xa, xb, seeds)
    out, grad, q_value, r_value, share = pl.pallas_call(
        outside_kernel,
        out_shape=[shape(19, N * N, NZ), shape(9, 1, 1, SEEDS)] + [shape(1, 1, SEEDS)] * 3,
        in_specs=[VM, VM, ANY] + [VM] * 6,
        out_specs=[ANY] + [VM] * 4,
        scratch_shapes=[
            vmem((2, PAD_LEN, NZ), F32),
            vmem((2, 19, T_LEN, NZ), F32),
            vmem((2, N_A, T_LEN, NZ), F32),
            vmem((2, 9, T_LEN, NZ), F32),
            vmem((19, N * N, NZ), F32),
            dma((2,)),
        ],
        compiler_params=params(),
        cost_estimate=cost(5_000_000, 8_000_000),
        name="outside",
    )(ya, yb, inside.reshape(19, N * N, NZ), fw, qw, pm, pick, hot, seeds)
    return out.reshape(19, N, N, NZ), grad, q_value, r_value, share


def solution(mesh):
    in_specs = (P(None, "gx", "gy", None), P("gx", "gy", None))
    out_specs = (
        P(None, "gx", "gy", None),
        P(None, "gx", "gy", None),
        P("gx", "gy", None),
        P("gx", "gy", None),
        P("gx", "gy", None),
    )
    return jax.shard_map(
        per_device, mesh=mesh, in_specs=in_specs, out_specs=out_specs, check_vma=False
    )
```

time: 180 us -> 58.6 us (0.33)
  starting transfers between devices: 92.4 us -> 28 us
  waiting for transfers between devices: 50.2 us -> 14.1 us
  local copies, waits for them, and re-layouts: 23.1 us -> 1.7 us
  Pallas kernels: 0 us -> 13.8 us
  other arithmetic: 11.7 us -> 0 us
    ppermute x12 -> x4, starting transfers between devices: 92.4 us -> 28 us  [the longest x1 13.3 us: per_device(): xb = lax.ppermute(xb, 'gx', x_second)]
    ppermute x12 -> x4, waiting for transfers between devices: 50.2 us -> 14.1 us  [the longest x1 7.24 us: per_device(): yb = lax.ppermute(yb, 'gy', y_second)]
    pallas_call x0 -> x5, Pallas kernels: none -> 13.8 us  [the longest x1 8.75 us: per_device(): pl.pallas_call(inside_kernel, out_shape=[shape(19, N, N, NZ), shape(2, 14...]
    another operation x3 -> x0, local copies, waits for them, and re-layouts: 11.8 us -> none  [the longest x2 11.8 us: per_device(): tensor = jnp.stack(comps).reshape(9, -1)]
    gather x1 -> x0, local copies, waits for them, and re-layouts: 6.41 us -> none  [per_device(): picked = jnp.take(tensor, seed_cells.reshape(-1), axis=1)]
    unnamed x38 -> x0, other arithmetic: 5.81 us -> none
    slice x43 -> x0, local copies, waits for them, and re-layouts: 2.65 us -> none  [the longest x40 2.19 us: shifted(): return jnp.roll(piece, VELOCITIES[index][2], axis=2)]
    mul x9 -> x0, other arithmetic: 2.41 us -> none  [the longest x2 1.35 us: per_device(): comps.append((rimmed[row, 2:, 1:-1] - rimmed[row, :-2, 1:-1]) * DIFF_SCALE)]
  transfers between devices with their start and end apart: 12 -> 4, of which waited for: 10 -> 2; matrix products, arithmetic and copies ran while one was open for 1% -> 0% of each run, Pallas kernels for 0% -> 16%
where the time goes in v1:
time: 58.6 us; the launch traced here: 58.4 us
  starting transfers between devices  28 us (48%)
  waiting for transfers between devices  14.1 us (24%)
  Pallas kernels  13.8 us (24%)
  local copies, waits for them, and re-layouts  1.7 us (3%)
  between operations  0.73 us (1%)
    ppermute x1, starting transfers between devices, per_device(): xb = lax.ppermute(xb, 'gx', x_second)  13.3 us
    ppermute x1, starting transfers between devices, per_device(): yb = lax.ppermute(yb, 'gy', y_second)  10.1 us
    pallas_call x1, Pallas kernels, per_device(): pl.pallas_call(inside_kernel, out_shape=[shape(19, N, N, NZ), shape(2, 14...  8.75 us
    ppermute x1, waiting for transfers between devices, per_device(): yb = lax.ppermute(yb, 'gy', y_second)  7.24 us
    ppermute x1, waiting for transfers between devices, per_device(): xb = lax.ppermute(xb, 'gx', x_second)  6.9 us
    pallas_call x1, Pallas kernels, per_device(): pl.pallas_call(outside_kernel, out_shape=[shape(19, N * N, NZ), shape(9,...  3.43 us
    ppermute x1, starting transfers between devices, per_device(): ya = lax.ppermute(ya, 'gy', y_first)  2.73 us
    ppermute x1, starting transfers between devices, per_device(): xa = lax.ppermute(xa, 'gx', x_first)  1.92 us
  transfers between devices with their start and end apart: 4, of which 2 were waited for; matrix products, arithmetic and copies ran while one was open for 0% of the time, Pallas kernels for 16%

profile of v1, /device:TPU:30, one launch (start us, length us, event | category | flops | bytes accessed | tf_op | source)
XLA Modules:
  0.0 58.4 jit_solution(7462532781060766492)
XLA Ops:
  0.6 0.0 copy-start
  0.6 1.7 %copy-done = f32[19,16,16,128]{3,2,1,0:T(8,128)S(1)} copy-done((f32[19,16,16,128]{3,2,1,0:T(8,128)S(1)}, f32[19,16,16,128]{3,2,1,0:T(8,128)}, u32[]{:S(2)}) %copy-start) | copy-done | bytes 2490392
  2.3 0.4 x_pack.1
  2.8 1.9 %collective-permute-start = (f32[38,16,128]{2,1,0:T(8,128)S(1)}, f32[38,16,128]{2,1,0:T(8,128)S(1)}, u32[]{:S(2)}, u32[]{:S(2)}) collective-permute-start(f32[38,16,128]{2,1,0:T(8,128)S(1)} %get-tuple-element.20), channel_id=1, source_target_pairs={{0,32},{32,0},{64,96},{96,64},{128,160},{160,128},{192,224},{224,1... | collective-permute-start | bytes 933896 | tf_op jit(solution)/shard_map/ppermute | solution.py:509
  4.7 13.3 %collective-permute-start.1 = (f32[38,16,128]{2,1,0:T(8,128)S(1)}, f32[38,16,128]{2,1,0:T(8,128)S(1)}, u32[]{:S(2)}, u32[]{:S(2)}) collective-permute-start(f32[38,16,128]{2,1,0:T(8,128)S(1)} %get-tuple-element.21), channel_id=1, source_target_pairs={{32,64},{64,32},{96,128},{128,96},{160,192},{192,160},{224,256},{2... | collective-permute-start | bytes 933896 | tf_op jit(solution)/shard_map/ppermute | solution.py:508
  18.0 0.0 copy-start.1
  18.0 0.7 %end_rows.1.g_ref = f32[6,19,16,128]{3,2,1,0:T(8,128)S(1)} custom-call(f32[19,256,128]{2,1,0:T(8,128)S(1)} %bitcast.4), custom_call_target="tpu_custom_call" | custom-call | flops 5000000 | bytes 3500000 | tf_op jit(solution)/shard_map/end_rows/pallas_call | solution.py:510
  18.7 0.0 collective-permute-done.xa
  18.7 6.9 %collective-permute-done.1.xb = f32[38,16,128]{2,1,0:T(8,128)S(1)} collective-permute-done((f32[38,16,128]{2,1,0:T(8,128)S(1)}, f32[38,16,128]{2,1,0:T(8,128)S(1)}, u32[]{:S(2)}, u32[]{:S(2)}) %collective-permute-start.1) | collective-permute-done | bytes 311328 | tf_op jit(solution)/shard_map/ppermute | solution.py:508
  25.6 0.5 y_pack.1
  26.1 2.7 %collective-permute-start.2 = (f32[324,128]{1,0:T(8,128)S(1)}, f32[324,128]{1,0:T(8,128)S(1)}, u32[]{:S(2)}, u32[]{:S(2)}) collective-permute-start(f32[324,128]{1,0:T(8,128)S(1)} %get-tuple-element.22), channel_id=1, source_target_pairs={{0,1},{1,0},{2,3},{3,2},{4,5},{5,4},{6,7},{7,6},{8,9},{9,8},{10,11... | collective-permute-start | bytes 497672 | tf_op jit(solution)/shard_map/ppermute | solution.py:535
  28.9 10.1 %collective-permute-start.3 = (f32[324,128]{1,0:T(8,128)S(1)}, f32[324,128]{1,0:T(8,128)S(1)}, u32[]{:S(2)}, u32[]{:S(2)}) collective-permute-start(f32[324,128]{1,0:T(8,128)S(1)} %get-tuple-element.23), channel_id=1, source_target_pairs={{1,2},{2,1},{3,4},{4,3},{5,6},{6,5},{7,8},{8,7},{9,10},{10,9},{11,... | collective-permute-start | bytes 497672 | tf_op jit(solution)/shard_map/ppermute | solution.py:534
  38.9 0.0 copy-done.1
  38.9 8.8 %inside.1 = (f32[19,16,16,128]{3,2,1,0:T(8,128)S(1)}, f32[2,14,24,128]{3,2,1,0:T(8,128)S(1)}, f32[2,4,24,128]{3,2,1,0:T(8,128)S(1)}, f32[4,4,24,128]{3,2,1,0:T(8...) custom-call(f32[19,16,16,128]{3,2,1,0:T(8,128)} %f_ref.1, f32[6,19,16,128]{3,2,1,0:T(8,128)S(1)} %end_rows.1.g_ref, ...), custom_call_target="tpu_custom_call" | custom-call | flops 50000000 | bytes 30000000 | tf_op jit(solution)/shard_map/inside/pallas_call | solution.py:536
  47.7 0.0 collective-permute-done.2.ya
  47.7 7.2 %collective-permute-done.3.yb = f32[324,128]{1,0:T(8,128)S(1)} collective-permute-done((f32[324,128]{1,0:T(8,128)S(1)}, f32[324,128]{1,0:T(8,128)S(1)}, u32[]{:S(2)}, u32[]{:S(2)}) %collective-permute-start.3) | collective-permute-done | bytes 165920 | tf_op jit(solution)/shard_map/ppermute | solution.py:534
  54.9 3.4 %outside.1 = (f32[19,256,128]{2,1,0:T(8,128)}, f32[9,1,1,128]{3,2,1,0:T(1,128)}, f32[1,1,128]{2,1,0:T(1,128)}, f32[1,1,128]{2,1,0:T(1,128)}, f32[1,1,128]{2,1,0:T(1,128)}) custom-call(f32[324,128]{1,0:T(8,128)S(1)} %collective-permute-done.2.ya, f32[324,128]{1,0:T(8,128)S(1)} %collective-permute-done.3.yb, f32[19,256,128]{2,1,0:T(8,128)S(1)} %bitcast.5, ...), custom_call_target="tpu_custom_call" | custom-call | flops 5000000 | bytes 8000000 | tf_op jit(solution)/shard_map/outside/pallas_call | solution.py:559
Async XLA Ops:
  0.6 1.7 %copy-start = (f32[19,16,16,128]{3,2,1,0:T(8,128)S(1)}, f32[19,16,16,128]{3,2,1,0:T(8,128)}, u32[]{:S(2)}) copy-start(f32[19,16,16,128]{3,2,1,0:T(8,128)} %f_ref.1) | copy-start | bytes 7471108
  2.8 15.9 %collective-permute-start = (f32[38,16,128]{2,1,0:T(8,128)S(1)}, f32[38,16,128]{2,1,0:T(8,128)S(1)}, u32[]{:S(2)}, u32[]{:S(2)}) collective-permute-start(f32[38,16,128]{2,1,0:T(8,128)S(1)} %get-tuple-element.20), channel_id=1, source_target_pairs={{0,32},{32,0},{64,96},{96,64},{128,160},{160,128},{192,224},{224,1... | collective-permute-start | bytes 933896 | tf_op jit(solution)/shard_map/ppermute | solution.py:509
  4.7 20.9 %collective-permute-start.1 = (f32[38,16,128]{2,1,0:T(8,128)S(1)}, f32[38,16,128]{2,1,0:T(8,128)S(1)}, u32[]{:S(2)}, u32[]{:S(2)}) collective-permute-start(f32[38,16,128]{2,1,0:T(8,128)S(1)} %get-tuple-element.21), channel_id=1, source_target_pairs={{32,64},{64,32},{96,128},{128,96},{160,192},{192,160},{224,256},{2... | collective-permute-start | bytes 933896 | tf_op jit(solution)/shard_map/ppermute | solution.py:508
  18.0 21.0 %copy-start.1 = (s32[1,1,128]{2,1,0:T(1,128)S(1)}, s32[1,1,128]{2,1,0:T(1,128)}, u32[]{:S(2)}) copy-start(s32[1,1,128]{2,1,0:T(1,128)} %param.3) | copy-start | bytes 1540
  26.1 21.6 %collective-permute-start.2 = (f32[324,128]{1,0:T(8,128)S(1)}, f32[324,128]{1,0:T(8,128)S(1)}, u32[]{:S(2)}, u32[]{:S(2)}) collective-permute-start(f32[324,128]{1,0:T(8,128)S(1)} %get-tuple-element.22), channel_id=1, source_target_pairs={{0,1},{1,0},{2,3},{3,2},{4,5},{5,4},{6,7},{7,6},{8,9},{9,8},{10,11... | collective-permute-start | bytes 497672 | tf_op jit(solution)/shard_map/ppermute | solution.py:535
  28.9 26.1 %collective-permute-start.3 = (f32[324,128]{1,0:T(8,128)S(1)}, f32[324,128]{1,0:T(8,128)S(1)}, u32[]{:S(2)}, u32[]{:S(2)}) collective-permute-start(f32[324,128]{1,0:T(8,128)S(1)} %get-tuple-element.23), channel_id=1, source_target_pairs={{1,2},{2,1},{3,4},{4,3},{5,6},{6,5},{7,8},{8,7},{9,10},{10,9},{11,... | collective-permute-start | bytes 497672 | tf_op jit(solution)/shard_map/ppermute | solution.py:534

commit v2 on v1

--- a/solution.py
+++ b/solution.py
@@ -48,7 +48,8 @@
 Y_LEN = S_OFF + 4 * N
 PAD_LEN = 336
 V_ROWS = (-1, 0, 1, 14, 15, 16)
-VMEM_LIMIT = 48 * 1024 * 1024
+UNROLL = 4
+VMEM_LIMIT = 28 * 1024 * 1024
 
 
 def x_fields(direction):
@@ -155,14 +156,21 @@
             pl.when(jnp.logical_not(first))(lambda put=put: put(b_out))
 
 
-def rows_kernel(f_ref, g_out):
+def rows_kernel(f_ref, seed_ref, g_out, inner_out, outer_out):
     for r, y in enumerate(OWN_ROWS):
         g = collide([f_ref[i, pl.ds(y, N, stride=N), :] for i in ALL])
         for i in ALL:
             g_out[r, i] = g[i]
-
-
-def y_pack_kernel(g_ref, xa, xb, a_out, b_out, lo, hi, t, hs):
+    xs, ys, _ = seed_parts(seed_ref[...])
+    row = lax.broadcasted_iota(jnp.int32, ((N + 2) * N, 1), 0)
+    inner_out[...] = one_hots(lax.div(row, N) - 1, lax.rem(row, N), xs, ys)
+    row = lax.broadcasted_iota(jnp.int32, (6 * WIDE, 1), 0)
+    block = lax.div(row, WIDE)
+    ry = jnp.where(block < 3, block - 1, block + 11)
+    outer_out[...] = one_hots(lax.rem(row, WIDE) - 2, ry, xs, ys)
+
+
+def y_pack_kernel(g_ref, xb, xa, a_out, b_out, t, lo, hi, hs):
     even_x = lax.rem(lax.axis_index("gx"), 2) == 0
     even_y = lax.rem(lax.axis_index("gy"), 2) == 0
 
@@ -269,7 +277,7 @@
     return out
 
 
-def inside_kernel(f_ref, g_ref, xa, xb, seed_ref, f_out, fw_out, qw_out, pm_out, pick_out, hot_out, g, h, t, m, v):
+def inside_kernel(f_ref, t, xa, xb, hots, seed_ref, f_out, fw_out, qw_out, pm_out, pick_out, g, h, m, v):
     even_x = lax.rem(lax.axis_index("gx"), 2) == 0
 
     def halo(x_hi, x_lo):
@@ -281,61 +289,6 @@
     pl.when(even_x)(lambda: halo(xa, xb))
     pl.when(jnp.logical_not(even_x))(lambda: halo(xb, xa))
 
-    def first(x, _):
-        out = collide([f_ref[i, x] for i in ALL])
-        for i in ALL:
-            g[i, x + 3] = out[i]
-        return 0
-
-    lax.fori_loop(0, N, first, 0)
-    inner = lax.broadcasted_iota(jnp.int32, (N, NZ), 0)
-    inner = (inner >= 1) & (inner <= N - 2)
-
-    def shift(value, i):
-        if C[i][1]:
-            value = pltpu.roll(value, C[i][1] % N, axis=0)
-        return zroll(value, C[i][2])
-
-    def second(x, _):
-        f = [shift(g[i, x + 1 - C[i][0]], i) for i in ALL]
-        out = collide(f)
-        for i in ALL:
-            h[i, x] = jnp.where(inner, out[i], 0.0)
-        return 0
-
-    lax.fori_loop(0, N + 4, second, 0)
-    iy = lax.broadcasted_iota(jnp.int32, (N, NZ), 0)
-    whole = (iy >= 2) & (iy <= N - 3)
-
-    def third(x, _):
-        got = [shift(h[i, x + 1 - C[i][0]], i) for i in ALL]
-
-        @pl.when((x >= 1) & (x <= N))
-        def _():
-            for i in ALL:
-                f_out[i, x - 1] = got[i]
-
-        mom = moments(got)
-        for k in range(4):
-            m[k, pl.ds(x * N, N)] = mom[k]
-        for k in range(3):
-            v[k, pl.ds(x * N, N)] = jnp.where(whole, mom[k + 1] / mom[0], 0.0)
-        return 0
-
-    lax.fori_loop(0, N + 2, third, 0)
-    pm_out[...] = jnp.ones_like(pm_out)
-    for r, y in enumerate((0, 1, 14, 15)):
-        for k in range(4):
-            pm_out[r, k, pl.ds(1, N + 2)] = m[k, pl.ds(y, N + 2, stride=N), :]
-
-    t[...] = jnp.ones_like(t)
-    for r, y in enumerate(OWN_ROWS):
-        if y in (2, 13):
-            continue
-        for i in ALL:
-            t[r, i, pl.ds(T_AT, N)] = g_ref[r, i]
-            for at in (-3, -2, -1, N, N + 1, N + 2):
-                t[r, i, pl.ds(T_AT + at, 1)] = g[i, at + 3, pl.ds(y, 1)]
     for side, s in ((0, 1), (1, -1)):
         rows = [OWN_ROWS.index(y) for y in ROWS[side]]
         toward, par, away = side_parts(s)
@@ -350,23 +303,62 @@
         for k, value in enumerate(moments(leave, away)):
             qw_out[side, k] = value
 
-    xs, ys, zs = seed_parts(seed_ref[...])
-    row = lax.broadcasted_iota(jnp.int32, ((N + 2) * N, 1), 0)
-    hots = one_hots(lax.div(row, N) - 1, lax.rem(row, N), xs, ys)
-    got = picks([v[k] for k in range(3)], hots, zs)
+    def first(x, _):
+        out = collide([f_ref[i, pl.ds(pl.multiple_of(x * N, N), N)] for i in ALL])
+        for i in ALL:
+            g[i, x + 3] = out[i]
+        return 0
+
+    lax.fori_loop(0, N, first, 0, unroll=UNROLL)
+    inner = lax.broadcasted_iota(jnp.int32, (N, NZ), 0)
+    inner = (inner >= 1) & (inner <= N - 2)
+
+    def shift(value, i):
+        if C[i][1]:
+            value = pltpu.roll(value, C[i][1] % N, axis=0)
+        return zroll(value, C[i][2])
+
+    def second(x, _):
+        f = [shift(g[i, x + 1 - C[i][0]], i) for i in ALL]
+        out = collide(f)
+        for i in ALL:
+            h[i, x] = jnp.where(inner, out[i], 0.0)
+        return 0
+
+    lax.fori_loop(0, N + 4, second, 0, unroll=UNROLL)
+    iy = lax.broadcasted_iota(jnp.int32, (N, NZ), 0)
+    whole = (iy >= 2) & (iy <= N - 3)
+
+    def third(x, _):
+        got = [shift(h[i, x + 1 - C[i][0]], i) for i in ALL]
+
+        @pl.when((x >= 1) & (x <= N))
+        def _():
+            for i in ALL:
+                f_out[i, x - 1] = got[i]
+
+        mom = moments(got)
+        for k in range(4):
+            m[k, pl.ds(x * N, N)] = mom[k]
+        for k in range(3):
+            v[k, pl.ds(x * N, N)] = jnp.where(whole, mom[k + 1] / mom[0], 0.0)
+        return 0
+
+    lax.fori_loop(0, N + 2, third, 0, unroll=UNROLL)
+    pm_out[...] = jnp.ones_like(pm_out)
+    for r, y in enumerate((0, 1, 14, 15)):
+        for k in range(4):
+            pm_out[r, k, pl.ds(1, N + 2)] = m[k, pl.ds(y, N + 2, stride=N), :]
+
+    zs = lax.rem(seed_ref[...], NZ)
+    got = picks([v[k] for k in range(3)], hots[...], zs)
     for k in range(9):
         pick_out[pl.ds(k, 1)] = got[k]
-    row = lax.broadcasted_iota(jnp.int32, (6 * WIDE, 1), 0)
-    block = lax.div(row, WIDE)
-    ry = jnp.where(block < 3, block - 1, block + 11)
-    hot_out[...] = one_hots(lax.rem(row, WIDE) - 2, ry, xs, ys)
 
 
 def outside_kernel(
-    ya, yb, f_hbm, fw, qw, pm, pick, hot, seed_ref, out_hbm, grad_out, q_out, r_out, s_out, msg, hs, hp, ep, fs, sems
+    yb, ya, f_in, fw, qw, pm, pick, hot, seed_ref, out_hbm, grad_out, q_out, r_out, s_out, msg, hs, hp, ep, fs, sems
 ):
-    fetch = pltpu.make_async_copy(f_hbm, fs, sems.at[0])
-    fetch.start()
     even_y = lax.rem(lax.axis_index("gy"), 2) == 0
 
     @pl.when(even_y)
@@ -437,11 +429,14 @@
             inv = 1.0 / total[0]
             vel[y] = [jnp.where(ok, total[k + 1] * inv, 0.0) for k in range(3)]
 
-    fetch.wait()
-    for i, y, value in patches:
-        fs[i, pl.ds(y, N, stride=N), :] = value[2 : 2 + N]
-    store = pltpu.make_async_copy(fs, out_hbm, sems.at[1])
-    store.start()
+    stores = []
+    for i in ALL:
+        fs[i] = f_in[i]
+        for k, y, value in patches:
+            if k == i:
+                fs[i, pl.ds(y, N, stride=N), :] = value[2 : 2 + N]
+        stores.append(pltpu.make_async_copy(fs.at[i], out_hbm.at[i], sems.at[i]))
+        stores[-1].start()
     zs = lax.rem(seed_ref[...], NZ)
     got = picks([jnp.concatenate([vel[y][k] for y in V_ROWS], axis=0) for k in range(3)], hot[...], zs)
     comps = [(got[k] + pick[pl.ds(k, 1)]) * SCALE for k in range(9)]
@@ -459,7 +454,8 @@
     q_out[0] = q
     r_out[0] = -(1.0 / 3.0) * r_sum
     s_out[0] = 2.0 * q / (norm + 0.25)
-    store.wait()
+    for store in stores:
+        store.wait()
 
 
 def swaps(count):
@@ -507,33 +503,36 @@
     )(populations)
     xb = lax.ppermute(xb, "gx", x_second)
     xa = lax.ppermute(xa, "gx", x_first)
-    g_rows = pl.pallas_call(
+    g_rows, hot_in, hot = pl.pallas_call(
         rows_kernel,
-        out_shape=shape(6, 19, N, NZ),
-        in_specs=[VM],
-        out_specs=VM,
+        out_shape=[
+            shape(6, 19, N, NZ),
+            jax.ShapeDtypeStruct(((N + 2) * N, 3 * SEEDS), BF16),
+            jax.ShapeDtypeStruct((6 * WIDE, 3 * SEEDS), BF16),
+        ],
+        in_specs=[VM] * 2,
+        out_specs=[VM] * 3,
         compiler_params=params(),
         cost_estimate=cost(5_000_000, 3_500_000),
         name="end_rows",
-    )(flat)
-    ya, yb = pl.pallas_call(
+    )(flat, seeds)
+    ya, yb, t = pl.pallas_call(
         y_pack_kernel,
-        out_shape=[shape(Y_LEN, NZ)] * 2,
+        out_shape=[shape(Y_LEN, NZ)] * 2 + [shape(6, 19, T_LEN, NZ)],
         in_specs=[VM] * 3,
-        out_specs=[VM] * 2,
+        out_specs=[VM] * 3,
         scratch_shapes=[
             vmem((X_LEN, N, NZ), F32),
             vmem((X_LEN, N, NZ), F32),
-            vmem((6, 19, T_LEN, NZ), F32),
             vmem((2, N_A, T_LEN, NZ), F32),
         ],
         compiler_params=params(),
         cost_estimate=cost(5_000_000, 2_000_000),
         name="y_pack",
-    )(g_rows, xa, xb)
+    )(g_rows, xb, xa)
     yb = lax.ppermute(yb, "gy", y_second)
     ya = lax.ppermute(ya, "gy", y_first)
-    inside, fw, qw, pm, pick, hot = pl.pallas_call(
+    inside, fw, qw, pm, pick = pl.pallas_call(
         inside_kernel,
         out_shape=[
             shape(19, N, N, NZ),
@@ -541,25 +540,23 @@
             shape(2, 4, WIDE, NZ),
             shape(4, 4, WIDE, NZ),
             shape(9, SEEDS),
-            jax.ShapeDtypeStruct((6 * WIDE, 3 * SEEDS), BF16),
         ],
-        in_specs=[VM] * 5,
-        out_specs=[VM] * 6,
+        in_specs=[VM] * 6,
+        out_specs=[VM] * 5,
         scratch_shapes=[
             vmem((19, N + 6, N, NZ), F32),
             vmem((19, N + 4, N, NZ), F32),
-            vmem((6, 19, T_LEN, NZ), F32),
             vmem((4, (N + 2) * N, NZ), F32),
             vmem((3, (N + 2) * N, NZ), F32),
         ],
         compiler_params=params(),
         cost_estimate=cost(50_000_000, 30_000_000),
         name="inside",
-    )(populations, g_rows, xa, xb, seeds)
+    )(flat, t, xa, xb, hot_in, seeds)
     out, grad, q_value, r_value, share = pl.pallas_call(
         outside_kernel,
         out_shape=[shape(19, N * N, NZ), shape(9, 1, 1, SEEDS)] + [shape(1, 1, SEEDS)] * 3,
-        in_specs=[VM, VM, ANY] + [VM] * 6,
+        in_specs=[VM] * 9,
         out_specs=[ANY] + [VM] * 4,
         scratch_shapes=[
             vmem((2, PAD_LEN, NZ), F32),
@@ -567,12 +564,12 @@
             vmem((2, N_A, T_LEN, NZ), F32),
             vmem((2, 9, T_LEN, NZ), F32),
             vmem((19, N * N, NZ), F32),
-            dma((2,)),
+            dma((19,)),
         ],
         compiler_params=params(),
         cost_estimate=cost(5_000_000, 8_000_000),
         name="outside",
-    )(ya, yb, inside.reshape(19, N * N, NZ), fw, qw, pm, pick, hot, seeds)
+    )(yb, ya, inside.reshape(19, N * N, NZ), fw, qw, pm, pick, hot, seeds)
     return out.reshape(19, N, N, NZ), grad, q_value, r_value, share
 
 

time: 58.6 us -> 52.7 us (0.90)
  Pallas kernels: 13.8 us -> 9.68 us
  starting transfers between devices: 28 us -> 27 us
  waiting for transfers between devices: 14.1 us -> 13.3 us
    pallas_call x1, Pallas kernels: 8.75 us -> 5.31 us  [per_device(): pl.pallas_call(inside_kernel, out_shape=[shape(19, N, N, NZ), shape(2, 14...]
    ppermute x1, waiting for transfers between devices: 6.9 us -> 4.27 us  [per_device(): xb = lax.ppermute(xb, 'gx', x_second)]
    ppermute x1, waiting for transfers between devices: 7.24 us -> 9.01 us  [per_device(): yb = lax.ppermute(yb, 'gy', y_second)]
    pallas_call x1, Pallas kernels: 3.43 us -> 2.48 us  [per_device(): pl.pallas_call(outside_kernel, out_shape=[shape(19, N * N, NZ), shape(9,...]
    ppermute x1, starting transfers between devices: 2.73 us -> 1.92 us  [per_device(): ya = lax.ppermute(ya, 'gy', y_first)]
    unnamed x4 -> x6, local copies, waits for them, and re-layouts: 1.7 us -> 1.71 us
  transfers between devices with their start and end apart: 4 -> 4, of which waited for: 2 -> 2; matrix products, arithmetic and copies ran while one was open for 0% -> 0% of each run, Pallas kernels for 16% -> 12%
where the time goes in v2:
time: 52.7 us; the launch traced here: 52.4 us
  starting transfers between devices  27 us (51%)
  waiting for transfers between devices  13.3 us (25%)
  Pallas kernels  9.68 us (18%)
  local copies, waits for them, and re-layouts  1.71 us (3%)
  between operations  0.72 us (1%)
    ppermute x1, starting transfers between devices, per_device(): xb = lax.ppermute(xb, 'gx', x_second)  12.7 us
    ppermute x1, starting transfers between devices, per_device(): yb = lax.ppermute(yb, 'gy', y_second)  10.4 us
    ppermute x1, waiting for transfers between devices, per_device(): yb = lax.ppermute(yb, 'gy', y_second)  9.01 us
    pallas_call x1, Pallas kernels, per_device(): pl.pallas_call(inside_kernel, out_shape=[shape(19, N, N, NZ), shape(2, 14...  5.31 us
    ppermute x1, waiting for transfers between devices, per_device(): xb = lax.ppermute(xb, 'gx', x_second)  4.27 us
    pallas_call x1, Pallas kernels, per_device(): pl.pallas_call(outside_kernel, out_shape=[shape(19, N * N, NZ), shape(9,...  2.48 us
    ppermute x1, starting transfers between devices, per_device(): xa = lax.ppermute(xa, 'gx', x_first)  1.92 us
    ppermute x1, starting transfers between devices, per_device(): ya = lax.ppermute(ya, 'gy', y_first)  1.92 us
  transfers between devices with their start and end apart: 4, of which 2 were waited for; matrix products, arithmetic and copies ran while one was open for 0% of the time, Pallas kernels for 12%

profile of v2, /device:TPU:30, one launch (start us, length us, event | category | flops | bytes accessed | tf_op | source)
XLA Modules:
  0.0 52.4 jit_solution(18229882812501367092)
XLA Ops:
  0.6 0.0 copy-start
  0.6 1.7 %copy-done = f32[19,16,16,128]{3,2,1,0:T(8,128)S(1)} copy-done((f32[19,16,16,128]{3,2,1,0:T(8,128)S(1)}, f32[19,16,16,128]{3,2,1,0:T(8,128)}, u32[]{:S(2)}) %copy-start) | copy-done | bytes 2490392
  2.3 0.0 copy-start.2
  2.3 0.4 x_pack.1
  2.8 0.0 copy-start.1
  2.8 12.7 %collective-permute-start = (f32[38,16,128]{2,1,0:T(8,128)S(1)}, f32[38,16,128]{2,1,0:T(8,128)S(1)}, u32[]{:S(2)}, u32[]{:S(2)}) collective-permute-start(f32[38,16,128]{2,1,0:T(8,128)S(1)} %get-tuple-element.24), channel_id=1, source_target_pairs={{32,64},{64,32},{96,128},{128,96},{160,192},{192,160},{224,256},{2... | collective-permute-start | bytes 933896 | tf_op jit(solution)/shard_map/ppermute | solution.py:504
  15.5 1.9 %collective-permute-start.1 = (f32[38,16,128]{2,1,0:T(8,128)S(1)}, f32[38,16,128]{2,1,0:T(8,128)S(1)}, u32[]{:S(2)}, u32[]{:S(2)}) collective-permute-start(f32[38,16,128]{2,1,0:T(8,128)S(1)} %get-tuple-element.25), channel_id=1, source_target_pairs={{0,32},{32,0},{64,96},{96,64},{128,160},{160,128},{192,224},{224,1... | collective-permute-start | bytes 933896 | tf_op jit(solution)/shard_map/ppermute | solution.py:505
  17.5 0.0 copy-done.2
  17.5 0.9 %end_rows.1 = (f32[6,19,16,128]{3,2,1,0:T(8,128)S(1)}, bf16[288,384]{1,0:T(8,128)(2,1)S(1)}, bf16[144,384]{1,0:T(8,128)(2,1)S(1)}) custom-call(f32[19,256,128]{2,1,0:T(8,128)S(1)} %bitcast.4, s32[1,128]{1,0:T(1,128)S(1)} %bitcast.7), custom_call_target="tpu_custom_call" | custom-call | flops 5000000 | bytes 3500000 | tf_op jit(solution)/shard_map/end_rows/pallas_call | solution.py:506
  18.3 4.3 %collective-permute-done.xb = f32[38,16,128]{2,1,0:T(8,128)S(1)} collective-permute-done((f32[38,16,128]{2,1,0:T(8,128)S(1)}, f32[38,16,128]{2,1,0:T(8,128)S(1)}, u32[]{:S(2)}, u32[]{:S(2)}) %collective-permute-start) | collective-permute-done | bytes 311328 | tf_op jit(solution)/shard_map/ppermute | solution.py:504
  22.6 0.0 collective-permute-done.1.xa
  22.6 0.6 %y_pack.1 = (f32[324,128]{1,0:T(8,128)S(1)}, f32[324,128]{1,0:T(8,128)S(1)}, f32[6,19,40,128]{3,2,1,0:T(8,128)S(1)}) custom-call(f32[6,19,16,128]{3,2,1,0:T(8,128)S(1)} %get-tuple-element.23.g_ref, f32[38,16,128]{2,1,0:T(8,128)S(1)} %collective-permute-done.xb, f32[38,16,128]{2,1,0:T(8,128)S(1)} %collective-permute-done.1.xa), custom_call_target="tpu_custom_call" | custom-call | flops 5000000 | bytes 2000000 | tf_op jit(solution)/shard_map/y_pack/pallas_call | solution.py:519
  23.2 10.4 %collective-permute-start.2 = (f32[324,128]{1,0:T(8,128)S(1)}, f32[324,128]{1,0:T(8,128)S(1)}, u32[]{:S(2)}, u32[]{:S(2)}) collective-permute-start(f32[324,128]{1,0:T(8,128)S(1)} %get-tuple-element.26), channel_id=1, source_target_pairs={{1,2},{2,1},{3,4},{4,3},{5,6},{6,5},{7,8},{8,7},{9,10},{10,9},{11,... | collective-permute-start | bytes 497672 | tf_op jit(solution)/shard_map/ppermute | solution.py:533
  33.7 1.9 %collective-permute-start.3 = (f32[324,128]{1,0:T(8,128)S(1)}, f32[324,128]{1,0:T(8,128)S(1)}, u32[]{:S(2)}, u32[]{:S(2)}) collective-permute-start(f32[324,128]{1,0:T(8,128)S(1)} %get-tuple-element.27), channel_id=1, source_target_pairs={{0,1},{1,0},{2,3},{3,2},{4,5},{5,4},{6,7},{7,6},{8,9},{9,8},{10,11... | collective-permute-start | bytes 497672 | tf_op jit(solution)/shard_map/ppermute | solution.py:534
  35.6 0.0 copy-done.1
  35.6 5.3 %inside.1 = (f32[19,16,16,128]{3,2,1,0:T(8,128)S(1)}, f32[2,14,24,128]{3,2,1,0:T(8,128)S(1)}, f32[2,4,24,128]{3,2,1,0:T(8,128)S(1)}, f32[4,4,24,128]{3,2,1,0:T(8,128)S(1)}, f32[9,128]{1,0:T(8,128)S(1)}) custom-call(f32[19,256,128]{2,1,0:T(8,128)S(1)} %bitcast.5, f32[6,19,40,128]{3,2,1,0:T(8,128)S(1)} %get-tuple-element.28.t, ...), custom_call_target="tpu_custom_call" | custom-call | flops 50000000 | bytes 30000000 | tf_op jit(solution)/shard_map/inside/pallas_call | solution.py:535
  40.9 9.0 %collective-permute-done.2.yb = f32[324,128]{1,0:T(8,128)S(1)} collective-permute-done((f32[324,128]{1,0:T(8,128)S(1)}, f32[324,128]{1,0:T(8,128)S(1)}, u32[]{:S(2)}, u32[]{:S(2)}) %collective-permute-start.2) | collective-permute-done | bytes 165920 | tf_op jit(solution)/shard_map/ppermute | solution.py:533
  49.9 0.0 collective-permute-done.3.ya
  49.9 2.5 %outside.1 = (f32[19,256,128]{2,1,0:T(8,128)}, f32[9,1,1,128]{3,2,1,0:T(1,128)}, f32[1,1,128]{2,1,0:T(1,128)}, f32[1,1,128]{2,1,0:T(1,128)}, f32[1,1,128]{2,1,0:T(1,128)}) custom-call(f32[324,128]{1,0:T(8,128)S(1)} %collective-permute-done.2.yb, f32[324,128]{1,0:T(8,128)S(1)} %collective-permute-done.3.ya, f32[19,256,128]{2,1,0:T(8,128)S(1)} %bitcast.6, ...), custom_call_target="tpu_custom_call" | custom-call | flops 5000000 | bytes 8000000 | tf_op jit(solution)/shard_map/outside/pallas_call | solution.py:556
Async XLA Ops:
  0.6 1.7 %copy-start = (f32[19,16,16,128]{3,2,1,0:T(8,128)S(1)}, f32[19,16,16,128]{3,2,1,0:T(8,128)}, u32[]{:S(2)}) copy-start(f32[19,16,16,128]{3,2,1,0:T(8,128)} %f_hbm.1) | copy-start | bytes 7471108
  2.3 15.1 %copy-start.2 = (s32[1,1,128]{2,1,0:T(1,128)S(1)}, s32[1,1,128]{2,1,0:T(1,128)}, u32[]{:S(2)}) copy-start(s32[1,1,128]{2,1,0:T(1,128)} %param.3) | copy-start | bytes 1540
  2.8 32.8 %copy-start.1 = (f32[19,16,16,128]{3,2,1,0:T(8,128)S(1)}, f32[19,16,16,128]{3,2,1,0:T(8,128)}, u32[]{:S(2)}) copy-start(f32[19,16,16,128]{3,2,1,0:T(8,128)} %f_hbm.1) | copy-start | bytes 7471108
  2.8 19.8 %collective-permute-start = (f32[38,16,128]{2,1,0:T(8,128)S(1)}, f32[38,16,128]{2,1,0:T(8,128)S(1)}, u32[]{:S(2)}, u32[]{:S(2)}) collective-permute-start(f32[38,16,128]{2,1,0:T(8,128)S(1)} %get-tuple-element.24), channel_id=1, source_target_pairs={{32,64},{64,32},{96,128},{128,96},{160,192},{192,160},{224,256},{2... | collective-permute-start | bytes 933896 | tf_op jit(solution)/shard_map/ppermute | solution.py:504
  15.5 7.1 %collective-permute-start.1 = (f32[38,16,128]{2,1,0:T(8,128)S(1)}, f32[38,16,128]{2,1,0:T(8,128)S(1)}, u32[]{:S(2)}, u32[]{:S(2)}) collective-permute-start(f32[38,16,128]{2,1,0:T(8,128)S(1)} %get-tuple-element.25), channel_id=1, source_target_pairs={{0,32},{32,0},{64,96},{96,64},{128,160},{160,128},{192,224},{224,1... | collective-permute-start | bytes 933896 | tf_op jit(solution)/shard_map/ppermute | solution.py:505
  23.2 26.7 %collective-permute-start.2 = (f32[324,128]{1,0:T(8,128)S(1)}, f32[324,128]{1,0:T(8,128)S(1)}, u32[]{:S(2)}, u32[]{:S(2)}) collective-permute-start(f32[324,128]{1,0:T(8,128)S(1)} %get-tuple-element.26), channel_id=1, source_target_pairs={{1,2},{2,1},{3,4},{4,3},{5,6},{6,5},{7,8},{8,7},{9,10},{10,9},{11,... | collective-permute-start | bytes 497672 | tf_op jit(solution)/shard_map/ppermute | solution.py:533
  33.7 16.3 %collective-permute-start.3 = (f32[324,128]{1,0:T(8,128)S(1)}, f32[324,128]{1,0:T(8,128)S(1)}, u32[]{:S(2)}, u32[]{:S(2)}) collective-permute-start(f32[324,128]{1,0:T(8,128)S(1)} %get-tuple-element.27), channel_id=1, source_target_pairs={{0,1},{1,0},{2,3},{3,2},{4,5},{5,4},{6,7},{7,6},{8,9},{9,8},{10,11... | collective-permute-start | bytes 497672 | tf_op jit(solution)/shard_map/ppermute | solution.py:534

commit v3 on v2

--- a/solution.py
+++ b/solution.py
@@ -47,6 +47,7 @@
 S_OFF = 13 * YW
 Y_LEN = S_OFF + 4 * N
 PAD_LEN = 336
+FAR_LEN = 328
 V_ROWS = (-1, 0, 1, 14, 15, 16)
 UNROLL = 4
 VMEM_LIMIT = 28 * 1024 * 1024
@@ -158,8 +159,9 @@
 
 def rows_kernel(f_ref, seed_ref, g_out, inner_out, outer_out):
     for r, y in enumerate(OWN_ROWS):
-        g = collide([f_ref[i, pl.ds(y, N, stride=N), :] for i in ALL])
-        for i in ALL:
+        used = {2: side_parts(-1)[0], N - 3: side_parts(1)[0]}.get(y, ALL)
+        g = collide([f_ref[i, pl.ds(y, N, stride=N), :] for i in ALL], used)
+        for i in used:
             g_out[r, i] = g[i]
     xs, ys, _ = seed_parts(seed_ref[...])
     row = lax.broadcasted_iota(jnp.int32, ((N + 2) * N, 1), 0)
@@ -185,13 +187,17 @@
         lo[...] = xa[...]
 
     for r, y in enumerate(OWN_ROWS):
-        for i in ALL:
+        used = {2: side_parts(-1)[0], N - 3: side_parts(1)[0]}.get(y, ALL)
+        for i in used:
             t[r, i, pl.ds(T_AT, N)] = g_ref[r, i]
         for layer, i in x_fields(-1):
-            t[r, i, pl.ds(T_AT + N + layer, 1)] = hi[X_POS[-1][(layer, i)], pl.ds(y, 1)]
+            if i in used:
+                t[r, i, pl.ds(T_AT + N + layer, 1)] = hi[X_POS[-1][(layer, i)], pl.ds(y, 1)]
         for layer, i in x_fields(1):
-            t[r, i, pl.ds(T_AT - 1 - layer, 1)] = lo[X_POS[1][(layer, i)], pl.ds(y, 1)]
-
+            if i in used:
+                t[r, i, pl.ds(T_AT - 1 - layer, 1)] = lo[X_POS[1][(layer, i)], pl.ds(y, 1)]
+
+    b_out[pl.ds(Y_LEN, FAR_LEN - Y_LEN)] = jnp.zeros((FAR_LEN - Y_LEN, NZ), F32)
     for side, s in ((0, -1), (1, 1)):
         rows = [OWN_ROWS.index(y) for y in ROWS[side]]
         toward, par, away = side_parts(s)
@@ -262,17 +268,15 @@
     up = jnp.where(iz == lax.rem(zs + 1, NZ), 1.0, 0.0)
     down = jnp.where(iz == lax.rem(zs + NZ - 1, NZ), 1.0, 0.0)
     across = up - down
+    total = None
+    for part in split3(jnp.concatenate(v, axis=1)):
+        got = lax.dot_general(part, hots, (((0,), (0,)), ((), ())), preferred_element_type=F32)
+        total = got if total is None else total + got
     out = []
     for comp in range(3):
-        total = None
-        for part in split3(v[comp]):
-            got = lax.dot_general(
-                part, hots, (((0,), (0,)), ((), ())), preferred_element_type=F32
-            )
-            total = got if total is None else total + got
         for kind in range(3):
             mask = across if kind == 2 else here
-            piece = total[:, kind * SEEDS : (kind + 1) * SEEDS]
+            piece = total[comp * NZ : (comp + 1) * NZ, kind * SEEDS : (kind + 1) * SEEDS]
             out.append(jnp.sum(piece * mask, axis=0, keepdims=True))
     return out
 
@@ -356,106 +360,137 @@
         pick_out[pl.ds(k, 1)] = got[k]
 
 
-def outside_kernel(
-    yb, ya, f_in, fw, qw, pm, pick, hot, seed_ref, out_hbm, grad_out, q_out, r_out, s_out, msg, hs, hp, ep, fs, sems
-):
-    even_y = lax.rem(lax.axis_index("gy"), 2) == 0
-
-    @pl.when(even_y)
-    def _():
-        msg[1, pl.ds(0, Y_LEN)] = ya[...]
-        msg[0, pl.ds(0, Y_LEN)] = yb[...]
-
-    @pl.when(jnp.logical_not(even_y))
-    def _():
-        msg[1, pl.ds(0, Y_LEN)] = yb[...]
-        msg[0, pl.ds(0, Y_LEN)] = ya[...]
-
+def side_cells(side, msg, fw, qw, pm, hs, hp, ep, store):
     row_x = lax.broadcasted_iota(jnp.int32, (WIDE, NZ), 0) - 2
     near = (row_x >= -1) & (row_x <= N)
     own = (row_x >= 0) & (row_x < N)
+    s = -1 if side else 1
+    toward, par, away = side_parts(s)
+    end, before = (N - 1, N - 2) if side else (0, 1)
+
+    def field(k):
+        return msg[pl.ds(k * YW, WIDE)]
+
+    f = {i: field(k) for k, i in enumerate(toward)}
+    f.update({i: fw[side, k] for k, i in enumerate(par + away)})
+    out = collide(f)
+    for i in ALL:
+        hs[i, pl.ds(8, WIDE)] = out[i]
+    coming = {i: field(N_A + k) for k, i in enumerate(toward)}
+    mom = [
+        field(2 * N_A) + qw[side, 0],
+        field(2 * N_A + 1) + qw[side, 1],
+        moment(coming, 1, toward) + qw[side, 2],
+        field(2 * N_A + 2) + qw[side, 3],
+    ]
+    eq = equil(mom, toward + par)
+    for k, i in enumerate(toward):
+        hp[k, pl.ds(8, WIDE)] = KEEP * coming[i] + eq[i]
+    for k, i in enumerate(par):
+        ep[k, pl.ds(8, WIDE)] = eq[i]
+
+    def moved(ref, k, i):
+        return zroll(ref[k, pl.ds(8 - C[i][0], WIDE)], C[i][2])
+
+    last = {i: moved(hp, k, i) for k, i in enumerate(toward)}
+    last.update({i: moved(hs, i, i) for i in par})
+    second = {i: moved(hs, i, i) for i in toward}
+    store({i: [(end, last[i])] + ([(before, second[i])] if i in toward else []) for i in toward + par})
     vel = {}
-    patches = []
-    for side, s in ((0, 1), (1, -1)):
-        toward, par, away = side_parts(s)
-        end, before = (0, 1) if side == 0 else (N - 1, N - 2)
-
-        def field(k):
-            return msg[side, pl.ds(k * YW, WIDE)]
-
-        f = {i: field(k) for k, i in enumerate(toward)}
-        f.update({i: fw[side, k] for k, i in enumerate(par + away)})
-        out = collide(f)
-        for i in ALL:
-            hs[side, i, pl.ds(8, WIDE)] = out[i]
-        coming = {i: field(N_A + k) for k, i in enumerate(toward)}
-        mom = [
-            field(2 * N_A) + qw[side, 0],
-            field(2 * N_A + 1) + qw[side, 1],
-            moment(coming, 1, toward) + qw[side, 2],
-            field(2 * N_A + 2) + qw[side, 3],
-        ]
-        eq = equil(mom, toward + par)
-        for k, i in enumerate(toward):
-            hp[side, k, pl.ds(8, WIDE)] = KEEP * coming[i] + eq[i]
-        for k, i in enumerate(par):
-            ep[side, k, pl.ds(8, WIDE)] = eq[i]
-
-        def moved(ref, k, i):
-            return zroll(ref[side, k, pl.ds(8 - C[i][0], WIDE)], C[i][2])
-
-        last = {i: moved(hp, k, i) for k, i in enumerate(toward)}
-        last.update({i: moved(hs, i, i) for i in par})
-        second = {i: moved(hs, i, i) for i in toward}
-        for i in toward + par:
-            patches.append((i, end, last[i]))
-        for i in toward:
-            patches.append((i, before, second[i]))
-        beyond = {i: moved(hs, i, i) for i in away}
-        beyond.update({i: moved(ep, k, i) for k, i in enumerate(par)})
-
-        for y, base, terms, group, ok in (
-            (end, [pm[(3 if side else 0), k] for k in range(4)], last, toward + par, near),
-            (before, [pm[(2 if side else 1), k] for k in range(4)], second, toward, near),
-            (
-                end - s,
-                [msg[side, pl.ds(S_OFF + N * k - 2, WIDE)] for k in range(4)],
-                beyond,
-                away + par,
-                own,
-            ),
-        ):
-            total = [a + b for a, b in zip(base, moments(terms, group))]
-            inv = 1.0 / total[0]
-            vel[y] = [jnp.where(ok, total[k + 1] * inv, 0.0) for k in range(3)]
-
-    stores = []
-    for i in ALL:
-        fs[i] = f_in[i]
-        for k, y, value in patches:
-            if k == i:
-                fs[i, pl.ds(y, N, stride=N), :] = value[2 : 2 + N]
-        stores.append(pltpu.make_async_copy(fs.at[i], out_hbm.at[i], sems.at[i]))
-        stores[-1].start()
-    zs = lax.rem(seed_ref[...], NZ)
-    got = picks([jnp.concatenate([vel[y][k] for y in V_ROWS], axis=0) for k in range(3)], hot[...], zs)
-    comps = [(got[k] + pick[pl.ds(k, 1)]) * SCALE for k in range(9)]
-    q_sum = add_up(comps[3 * a + b] * comps[3 * b + a] for a in range(3) for b in range(3))
-    r_sum = add_up(
-        comps[3 * a + b] * comps[3 * b + c] * comps[3 * c + a]
-        for a in range(3)
-        for b in range(3)
-        for c in range(3)
-    )
-    norm = add_up(c * c for c in comps)
-    q = -0.5 * q_sum
-    for k in range(9):
-        grad_out[k, 0] = comps[k]
-    q_out[0] = q
-    r_out[0] = -(1.0 / 3.0) * r_sum
-    s_out[0] = 2.0 * q / (norm + 0.25)
-    for store in stores:
-        store.wait()
+    beyond = {i: moved(hs, i, i) for i in away}
+    beyond.update({i: moved(ep, k, i) for k, i in enumerate(par)})
+    for y, base, terms, group, ok in (
+        (end, [pm[(3 if side else 0), k] for k in range(4)], last, toward + par, near),
+        (before, [pm[(2 if side else 1), k] for k in range(4)], second, toward, near),
+        (end - s, [msg[pl.ds(S_OFF + N * k - 2, WIDE)] for k in range(4)], beyond, away + par, own),
+    ):
+        total = [a + b for a, b in zip(base, moments(terms, group))]
+        inv = 1.0 / total[0]
+        vel[y] = [jnp.where(ok, total[k + 1] * inv, 0.0) for k in range(3)]
+    return vel
+
+
+def half_out(i, side, f_in, fs, out_hbm, sems, patches):
+    for x in range(N):
+        fs[i, pl.ds(x * 8, 8)] = f_in[i, x, side]
+    for y, value in patches:
+        fs[i, pl.ds(y - 8 * side, N, stride=8), :] = value[2 : 2 + N]
+    copy = pltpu.make_async_copy(fs.at[i].reshape(N, 8, NZ), out_hbm.at[i, :, side], sems.at[i])
+    copy.start()
+    return copy
+
+
+def side_picks(side, vel, hot, zs):
+    rows = V_ROWS[3:] if side else V_ROWS[:3]
+    v = [jnp.concatenate([vel[y][k] for y in rows], axis=0) for k in range(3)]
+    return picks(v, hot[pl.ds(3 * WIDE * side, 3 * WIDE)], zs)
+
+
+def first_side_kernel(ya, f_in, fw, qw, pm, pick, hot, seed_ref, out_hbm, pick_out, msg, hs, hp, ep, fs, sems):
+    msg[pl.ds(0, Y_LEN)] = ya[...]
+
+    def work(side):
+        other = 1 - side
+        copies = [pltpu.make_async_copy(f_in.at[:, :, other], out_hbm.at[:, :, other], sems.at[19])]
+        copies[0].start()
+
+        def store(patches):
+            for i in ALL:
+                copies.append(half_out(i, side, f_in, fs, out_hbm, sems, patches.get(i, [])))
+
+        vel = side_cells(side, msg, fw, qw, pm, hs, hp, ep, store)
+        zs = lax.rem(seed_ref[...], NZ)
+        got = side_picks(side, vel, hot, zs)
+        for k in range(9):
+            pick_out[pl.ds(k, 1)] = got[k] + pick[pl.ds(k, 1)]
+        for copy in copies:
+            copy.wait()
+
+    even = lax.rem(lax.axis_index("gy"), 2) == 0
+    pl.when(even)(lambda: work(1))
+    pl.when(jnp.logical_not(even))(lambda: work(0))
+
+
+def second_side_kernel(
+    yb, fw, qw, pm, pick, hot, seed_ref, _, out_hbm, grad_out, q_out, r_out, s_out, msg, hs, hp, ep, rows, sems
+):
+    msg[pl.ds(0, FAR_LEN)] = yb[...]
+
+    def work(side):
+        copies = []
+
+        def store(patches):
+            for i, changed in patches.items():
+                for y, value in changed:
+                    k = len(copies)
+                    rows[k] = value[2 : 2 + N]
+                    copies.append(pltpu.make_async_copy(rows.at[k], out_hbm.at[i, :, y], sems.at[k]))
+                    copies[k].start()
+
+        vel = side_cells(side, msg, fw, qw, pm, hs, hp, ep, store)
+        zs = lax.rem(seed_ref[...], NZ)
+        got = side_picks(side, vel, hot, zs)
+        comps = [(got[k] + pick[pl.ds(k, 1)]) * SCALE for k in range(9)]
+        q_sum = add_up(comps[3 * a + b] * comps[3 * b + a] for a in range(3) for b in range(3))
+        r_sum = add_up(
+            comps[3 * a + b] * comps[3 * b + c] * comps[3 * c + a]
+            for a in range(3)
+            for b in range(3)
+            for c in range(3)
+        )
+        norm = add_up(c * c for c in comps)
+        q = -0.5 * q_sum
+        for k in range(9):
+            grad_out[k, 0] = comps[k]
+        q_out[0] = q
+        r_out[0] = -(1.0 / 3.0) * r_sum
+        s_out[0] = 2.0 * q / (norm + 0.25)
+        for copy in copies:
+            copy.wait()
+
+    even = lax.rem(lax.axis_index("gy"), 2) == 0
+    pl.when(even)(lambda: work(0))
+    pl.when(jnp.logical_not(even))(lambda: work(1))
 
 
 def swaps(count):
@@ -518,7 +553,7 @@
     )(flat, seeds)
     ya, yb, t = pl.pallas_call(
         y_pack_kernel,
-        out_shape=[shape(Y_LEN, NZ)] * 2 + [shape(6, 19, T_LEN, NZ)],
+        out_shape=[shape(Y_LEN, NZ), shape(FAR_LEN, NZ), shape(6, 19, T_LEN, NZ)],
         in_specs=[VM] * 3,
         out_specs=[VM] * 3,
         scratch_shapes=[
@@ -553,24 +588,35 @@
         cost_estimate=cost(50_000_000, 30_000_000),
         name="inside",
     )(flat, t, xa, xb, hot_in, seeds)
+    inside = inside.reshape(19, N, 2, 8, NZ)
+    side_scratch = [
+        vmem((PAD_LEN, NZ), F32),
+        vmem((19, T_LEN, NZ), F32),
+        vmem((N_A, T_LEN, NZ), F32),
+        vmem((9, T_LEN, NZ), F32),
+    ]
+    half, pick = pl.pallas_call(
+        first_side_kernel,
+        out_shape=[shape(19, N, 2, 8, NZ), shape(9, SEEDS)],
+        in_specs=[VM] * 8,
+        out_specs=[ANY, VM],
+        scratch_shapes=side_scratch + [vmem((19, N * 8, NZ), F32), dma((20,))],
+        compiler_params=params(),
+        cost_estimate=cost(5_000_000, 4_000_000),
+        name="first_side",
+    )(ya, inside, fw, qw, pm, pick, hot, seeds)
     out, grad, q_value, r_value, share = pl.pallas_call(
-        outside_kernel,
-        out_shape=[shape(19, N * N, NZ), shape(9, 1, 1, SEEDS)] + [shape(1, 1, SEEDS)] * 3,
-        in_specs=[VM] * 9,
+        second_side_kernel,
+        out_shape=[shape(19, N, N, NZ), shape(9, 1, 1, SEEDS)] + [shape(1, 1, SEEDS)] * 3,
+        in_specs=[VM] * 7 + [ANY],
         out_specs=[ANY] + [VM] * 4,
-        scratch_shapes=[
-            vmem((2, PAD_LEN, NZ), F32),
-            vmem((2, 19, T_LEN, NZ), F32),
-            vmem((2, N_A, T_LEN, NZ), F32),
-            vmem((2, 9, T_LEN, NZ), F32),
-            vmem((19, N * N, NZ), F32),
-            dma((19,)),
-        ],
+        scratch_shapes=side_scratch + [vmem((19, N, NZ), F32), dma((19,))],
+        input_output_aliases={7: 0},
         compiler_params=params(),
-        cost_estimate=cost(5_000_000, 8_000_000),
-        name="outside",
-    )(yb, ya, inside.reshape(19, N * N, NZ), fw, qw, pm, pick, hot, seeds)
-    return out.reshape(19, N, N, NZ), grad, q_value, r_value, share
+        cost_estimate=cost(5_000_000, 3_000_000),
+        name="second_side",
+    )(yb, fw, qw, pm, pick, hot, seeds, half.reshape(19, N, N, NZ))
+    return out, grad, q_value, r_value, share
 
 
 def solution(mesh):

time: 52.7 us -> 51.7 us (0.981)
  waiting for transfers between devices: 13.3 us -> 11.8 us
  Pallas kernels: 9.68 us -> 10.3 us
    ppermute x1, waiting for transfers between devices: 9.01 us -> 7.38 us  [per_device(): yb = lax.ppermute(yb, 'gy', y_second)]
    pallas_call x2 -> x3, Pallas kernels: 3.09 us -> 3.8 us  [the longest x1 1.62 us: per_device(): pl.pallas_call(second_side_kernel, out_shape=[shape(19, N, N, NZ), shape(...]
  transfers between devices with their start and end apart: 4 -> 4, of which waited for: 2 -> 2; matrix products, arithmetic and copies ran while one was open for 0% -> 0% of each run, Pallas kernels for 12% -> 15%
where the time goes in v3:
time: 51.7 us; the launch traced here: 51.5 us
  starting transfers between devices  27 us (52%)
  waiting for transfers between devices  11.8 us (23%)
  Pallas kernels  10.3 us (20%)
  local copies, waits for them, and re-layouts  1.71 us (3%)
  between operations  0.73 us (1%)
    ppermute x1, starting transfers between devices, per_device(): xb = lax.ppermute(xb, 'gx', x_second)  12.7 us
    ppermute x1, starting transfers between devices, per_device(): yb = lax.ppermute(yb, 'gy', y_second)  10.4 us
    ppermute x1, waiting for transfers between devices, per_device(): yb = lax.ppermute(yb, 'gy', y_second)  7.38 us
    pallas_call x1, Pallas kernels, per_device(): pl.pallas_call(inside_kernel, out_shape=[shape(19, N, N, NZ), shape(2, 14...  5.27 us
    ppermute x1, waiting for transfers between devices, per_device(): xb = lax.ppermute(xb, 'gx', x_second)  4.33 us
    ppermute x1, starting transfers between devices, per_device(): xa = lax.ppermute(xa, 'gx', x_first)  1.92 us
    ppermute x1, starting transfers between devices, per_device(): ya = lax.ppermute(ya, 'gy', y_first)  1.92 us
    unnamed x6, local copies, waits for them, and re-layouts  1.71 us
  transfers between devices with their start and end apart: 4, of which 2 were waited for; matrix products, arithmetic and copies ran while one was open for 0% of the time, Pallas kernels for 15%

profile of v3, /device:TPU:30, one launch (start us, length us, event | category | flops | bytes accessed | tf_op | source)
XLA Modules:
  0.0 51.5 jit_solution(3649815812781589489)
XLA Ops:
  0.6 0.0 copy-start
  0.6 1.7 %copy-done = f32[19,16,16,128]{3,2,1,0:T(8,128)S(1)} copy-done((f32[19,16,16,128]{3,2,1,0:T(8,128)S(1)}, f32[19,16,16,128]{3,2,1,0:T(8,128)}, u32[]{:S(2)}) %copy-start) | copy-done | bytes 2490392
  2.3 0.0 copy-start.2
  2.3 0.4 x_pack.1
  2.8 0.0 copy-start.1
  2.8 12.7 %collective-permute-start = (f32[38,16,128]{2,1,0:T(8,128)S(1)}, f32[38,16,128]{2,1,0:T(8,128)S(1)}, u32[]{:S(2)}, u32[]{:S(2)}) collective-permute-start(f32[38,16,128]{2,1,0:T(8,128)S(1)} %get-tuple-element.21), channel_id=1, source_target_pairs={{32,64},{64,32},{96,128},{128,96},{160,192},{192,160},{224,256},{2... | collective-permute-start | bytes 933896 | tf_op jit(solution)/shard_map/ppermute | solution.py:539
  15.5 1.9 %collective-permute-start.1 = (f32[38,16,128]{2,1,0:T(8,128)S(1)}, f32[38,16,128]{2,1,0:T(8,128)S(1)}, u32[]{:S(2)}, u32[]{:S(2)}) collective-permute-start(f32[38,16,128]{2,1,0:T(8,128)S(1)} %get-tuple-element.22), channel_id=1, source_target_pairs={{0,32},{32,0},{64,96},{96,64},{128,160},{160,128},{192,224},{224,1... | collective-permute-start | bytes 933896 | tf_op jit(solution)/shard_map/ppermute | solution.py:540
  17.5 0.0 copy-done.2
  17.5 0.8 %end_rows.1 = (f32[6,19,16,128]{3,2,1,0:T(8,128)S(1)}, bf16[288,384]{1,0:T(8,128)(2,1)S(1)}, bf16[144,384]{1,0:T(8,128)(2,1)S(1)}) custom-call(f32[19,256,128]{2,1,0:T(8,128)S(1)} %bitcast.4, s32[1,128]{1,0:T(1,128)S(1)} %bitcast.7), custom_call_target="tpu_custom_call" | custom-call | flops 5000000 | bytes 3500000 | tf_op jit(solution)/shard_map/end_rows/pallas_call | solution.py:541
  18.3 4.3 %collective-permute-done.xb = f32[38,16,128]{2,1,0:T(8,128)S(1)} collective-permute-done((f32[38,16,128]{2,1,0:T(8,128)S(1)}, f32[38,16,128]{2,1,0:T(8,128)S(1)}, u32[]{:S(2)}, u32[]{:S(2)}) %collective-permute-start) | collective-permute-done | bytes 311328 | tf_op jit(solution)/shard_map/ppermute | solution.py:539
  22.6 0.0 collective-permute-done.1.xa
  22.6 0.6 %y_pack.1 = (f32[324,128]{1,0:T(8,128)S(1)}, f32[328,128]{1,0:T(8,128)S(1)}, f32[6,19,40,128]{3,2,1,0:T(8,128)S(1)}) custom-call(f32[6,19,16,128]{3,2,1,0:T(8,128)S(1)} %get-tuple-element.20.g_ref, f32[38,16,128]{2,1,0:T(8,128)S(1)} %collective-permute-done.xb, f32[38,16,128]{2,1,0:T(8,128)S(1)} %collective-permute-done.1.xa), custom_call_target="tpu_custom_call" | custom-call | flops 5000000 | bytes 2000000 | tf_op jit(solution)/shard_map/y_pack/pallas_call | solution.py:554
  23.2 10.4 %collective-permute-start.2 = (f32[328,128]{1,0:T(8,128)S(1)}, f32[328,128]{1,0:T(8,128)S(1)}, u32[]{:S(2)}, u32[]{:S(2)}) collective-permute-start(f32[328,128]{1,0:T(8,128)S(1)} %get-tuple-element.23), channel_id=1, source_target_pairs={{1,2},{2,1},{3,4},{4,3},{5,6},{6,5},{7,8},{8,7},{9,10},{10,9},{11,... | collective-permute-start | bytes 503816 | tf_op jit(solution)/shard_map/ppermute | solution.py:568
  33.6 1.9 %collective-permute-start.3 = (f32[324,128]{1,0:T(8,128)S(1)}, f32[324,128]{1,0:T(8,128)S(1)}, u32[]{:S(2)}, u32[]{:S(2)}) collective-permute-start(f32[324,128]{1,0:T(8,128)S(1)} %get-tuple-element.29), channel_id=1, source_target_pairs={{0,1},{1,0},{2,3},{3,2},{4,5},{5,4},{6,7},{7,6},{8,9},{9,8},{10,11... | collective-permute-start | bytes 497672 | tf_op jit(solution)/shard_map/ppermute | solution.py:569
  35.5 0.0 copy-done.1
  35.6 5.3 %inside.1 = (f32[19,16,16,128]{3,2,1,0:T(8,128)S(1)}, f32[2,14,24,128]{3,2,1,0:T(8,128)S(1)}, f32[2,4,24,128]{3,2,1,0:T(8,128)S(1)}, f32[4,4,24,128]{3,2,1,0:T(8,128)S(1)}, f32[9,128]{1,0:T(8,128)S(1)}) custom-call(f32[19,256,128]{2,1,0:T(8,128)S(1)} %bitcast.5, f32[6,19,40,128]{3,2,1,0:T(8,128)S(1)} %get-tuple-element.24.t, ...), custom_call_target="tpu_custom_call" | custom-call | flops 50000000 | bytes 30000000 | tf_op jit(solution)/shard_map/inside/pallas_call | solution.py:570
  40.8 0.0 collective-permute-done.3.ya
  40.9 1.6 %first_side.1 = (f32[19,16,2,8,128]{4,3,2,1,0:T(8,128)}, f32[9,128]{1,0:T(8,128)S(1)}) custom-call(f32[324,128]{1,0:T(8,128)S(1)} %collective-permute-done.3.ya, f32[19,16,2,8,128]{4,3,2,1,0:T(8,128)S(1)} %bitcast.6, f32[2,14,24,128]{3,2,1,0:T(8,128)S(1)} %get-tuple-element.26.fw, f32[2,4,24,128]{3,2,1,0:T(8,128)S(1)} %get-tuple-element.27.qw, ...), custom_call_target="tpu_custom_call" | custom-call | flops 5000000 | bytes 4000000 | tf_op jit(solution)/shard_map/first_side/pallas_call | solution.py:598
  42.5 7.4 %collective-permute-done.2.yb = f32[328,128]{1,0:T(8,128)S(1)} collective-permute-done((f32[328,128]{1,0:T(8,128)S(1)}, f32[328,128]{1,0:T(8,128)S(1)}, u32[]{:S(2)}, u32[]{:S(2)}) %collective-permute-start.2) | collective-permute-done | bytes 167968 | tf_op jit(solution)/shard_map/ppermute | solution.py:568
  49.9 1.6 %second_side.1 = (f32[19,16,16,128]{3,2,1,0:T(8,128)}, f32[9,1,1,128]{3,2,1,0:T(1,128)}, f32[1,1,128]{2,1,0:T(1,128)}, f32[1,1,128]{2,1,0:T(1,128)}, f32[1,1,128]{2,1,0:T(1,128)}) custom-call(f32[328,128]{1,0:T(8,128)S(1)} %collective-permute-done.2.yb, f32[2,14,24,128]{3,2,1,0:T(8,128)S(1)} %get-tuple-element.26.fw, ...), custom_call_target="tpu_custom_call", output_to_operand_aliasing={{0}: (7, {})} | custom-call | flops 5000000 | bytes 3000000 | tf_op jit(solution)/shard_map/second_side/pallas_call | solution.py:608
Async XLA Ops:
  0.6 1.7 %copy-start = (f32[19,16,16,128]{3,2,1,0:T(8,128)S(1)}, f32[19,16,16,128]{3,2,1,0:T(8,128)}, u32[]{:S(2)}) copy-start(f32[19,16,16,128]{3,2,1,0:T(8,128)} %f_hbm.1) | copy-start | bytes 7471108
  2.3 15.1 %copy-start.2 = (s32[1,1,128]{2,1,0:T(1,128)S(1)}, s32[1,1,128]{2,1,0:T(1,128)}, u32[]{:S(2)}) copy-start(s32[1,1,128]{2,1,0:T(1,128)} %param.3) | copy-start | bytes 1540
  2.8 32.8 %copy-start.1 = (f32[19,16,16,128]{3,2,1,0:T(8,128)S(1)}, f32[19,16,16,128]{3,2,1,0:T(8,128)}, u32[]{:S(2)}) copy-start(f32[19,16,16,128]{3,2,1,0:T(8,128)} %f_hbm.1) | copy-start | bytes 7471108
  2.8 19.8 %collective-permute-start = (f32[38,16,128]{2,1,0:T(8,128)S(1)}, f32[38,16,128]{2,1,0:T(8,128)S(1)}, u32[]{:S(2)}, u32[]{:S(2)}) collective-permute-start(f32[38,16,128]{2,1,0:T(8,128)S(1)} %get-tuple-element.21), channel_id=1, source_target_pairs={{32,64},{64,32},{96,128},{128,96},{160,192},{192,160},{224,256},{2... | collective-permute-start | bytes 933896 | tf_op jit(solution)/shard_map/ppermute | solution.py:539
  15.5 7.1 %collective-permute-start.1 = (f32[38,16,128]{2,1,0:T(8,128)S(1)}, f32[38,16,128]{2,1,0:T(8,128)S(1)}, u32[]{:S(2)}, u32[]{:S(2)}) collective-permute-start(f32[38,16,128]{2,1,0:T(8,128)S(1)} %get-tuple-element.22), channel_id=1, source_target_pairs={{0,32},{32,0},{64,96},{96,64},{128,160},{160,128},{192,224},{224,1... | collective-permute-start | bytes 933896 | tf_op jit(solution)/shard_map/ppermute | solution.py:540
  23.2 26.7 %collective-permute-start.2 = (f32[328,128]{1,0:T(8,128)S(1)}, f32[328,128]{1,0:T(8,128)S(1)}, u32[]{:S(2)}, u32[]{:S(2)}) collective-permute-start(f32[328,128]{1,0:T(8,128)S(1)} %get-tuple-element.23), channel_id=1, source_target_pairs={{1,2},{2,1},{3,4},{4,3},{5,6},{6,5},{7,8},{8,7},{9,10},{10,9},{11,... | collective-permute-start | bytes 503816 | tf_op jit(solution)/shard_map/ppermute | solution.py:568
  33.6 7.3 %collective-permute-start.3 = (f32[324,128]{1,0:T(8,128)S(1)}, f32[324,128]{1,0:T(8,128)S(1)}, u32[]{:S(2)}, u32[]{:S(2)}) collective-permute-start(f32[324,128]{1,0:T(8,128)S(1)} %get-tuple-element.29), channel_id=1, source_target_pairs={{0,1},{1,0},{2,3},{3,2},{4,5},{5,4},{6,7},{7,6},{8,9},{9,8},{10,11... | collective-permute-start | bytes 497672 | tf_op jit(solution)/shard_map/ppermute | solution.py:569

commit v4 on v3

--- a/solution.py
+++ b/solution.py
@@ -133,20 +133,14 @@
     return toward, par, away
 
 
-def x_pack_kernel(f_hbm, a_out, b_out, buf, sems):
-    copies = [
-        pltpu.make_async_copy(f_hbm.at[:, pl.ds(start, 3)], buf.at[side], sems.at[side])
-        for side, start in ((0, 0), (1, N - 3))
-    ]
-    for copy in copies:
-        copy.start()
+def x_pack_kernel(low, high, a_out, b_out):
     even = lax.rem(lax.axis_index("gx"), 2) == 0
     for side, direction in ((0, -1), (1, 1)):
-        copies[side].wait()
+        buf = high if side else low
         for layer in range(3):
             at = layer if side == 0 else 2 - layer
             wanted = [i for i in ALL if (layer, i) in X_POS[direction]]
-            g = collide([buf[side, i, at] for i in ALL], wanted)
+            g = collide([buf[i, at] for i in ALL], wanted)
 
             def put(out, layer=layer, g=g, direction=direction):
                 for i, value in g.items():
@@ -529,13 +523,12 @@
     xa, xb = pl.pallas_call(
         x_pack_kernel,
         out_shape=[shape(X_LEN, N, NZ)] * 2,
-        in_specs=[ANY],
+        in_specs=[VM] * 2,
         out_specs=[VM] * 2,
-        scratch_shapes=[vmem((2, 19, 3, N, NZ), F32), dma((2,))],
         compiler_params=params(),
         cost_estimate=cost(5_000_000, 1_500_000),
         name="x_pack",
-    )(populations)
+    )(populations[:, :3], populations[:, N - 3 :])
     xb = lax.ppermute(xb, "gx", x_second)
     xa = lax.ppermute(xa, "gx", x_first)
     g_rows, hot_in, hot = pl.pallas_call(

time: 51.7 us -> 51.2 us (level)
    unnamed x6 -> x4, local copies, waits for them, and re-layouts: 1.71 us -> 0.01 us
    slice x0 -> x1, local copies, waits for them, and re-layouts: none -> 1.38 us  [per_device(): populations[:, N - 3:]]
  transfers between devices with their start and end apart: 4 -> 4, of which waited for: 2 -> 3; matrix products, arithmetic and copies ran while one was open for 0% -> 0% of each run, Pallas kernels for 15% -> 15%
where the time goes in v4:
time: 51.2 us; the launch traced here: 51 us
  starting transfers between devices  26.9 us (53%)
  waiting for transfers between devices  11.8 us (23%)
  Pallas kernels  10.2 us (20%)
  local copies, waits for them, and re-layouts  1.39 us (3%)
  between operations  0.74 us (1%)
    ppermute x1, starting transfers between devices, per_device(): xb = lax.ppermute(xb, 'gx', x_second)  12.6 us
    ppermute x1, starting transfers between devices, per_device(): yb = lax.ppermute(yb, 'gy', y_second)  10.4 us
    ppermute x1, waiting for transfers between devices, per_device(): yb = lax.ppermute(yb, 'gy', y_second)  7.38 us
    pallas_call x1, Pallas kernels, per_device(): pl.pallas_call(inside_kernel, out_shape=[shape(19, N, N, NZ), shape(2, 14...  5.26 us
    ppermute x1, waiting for transfers between devices, per_device(): xb = lax.ppermute(xb, 'gx', x_second)  4.32 us
    ppermute x1, starting transfers between devices, per_device(): ya = lax.ppermute(ya, 'gy', y_first)  1.92 us
    ppermute x1, starting transfers between devices, per_device(): xa = lax.ppermute(xa, 'gx', x_first)  1.92 us
    pallas_call x1, Pallas kernels, per_device(): pl.pallas_call(second_side_kernel, out_shape=[shape(19, N, N, NZ), shape(...  1.62 us
  transfers between devices with their start and end apart: 4, of which 3 were waited for; matrix products, arithmetic and copies ran while one was open for 0% of the time, Pallas kernels for 15%

profile of v4, /device:TPU:30, one launch (start us, length us, event | category | flops | bytes accessed | tf_op | source)
XLA Modules:
  0.0 51.0 jit_solution(605553180097126204)
XLA Ops:
  0.6 0.0 copy-start
  0.6 0.0 copy-start.1
  0.7 1.4 %fusion = (f32[19,3,16,128]{3,2,1,0:T(8,128)S(1)}, f32[19,3,16,128]{3,2,1,0:T(8,128)S(1)}) fusion(f32[19,16,16,128]{3,2,1,0:T(8,128)} %param.2), kind=kLoop, calls=%fused_computation | loop fusion | bytes 1867776 | tf_op jit(solution)/shard_map/slice | solution.py:531
  2.0 0.3 x_pack.1
  2.4 12.6 %collective-permute-start = (f32[38,16,128]{2,1,0:T(8,128)S(1)}, f32[38,16,128]{2,1,0:T(8,128)S(1)}, u32[]{:S(2)}, u32[]{:S(2)}) collective-permute-start(f32[38,16,128]{2,1,0:T(8,128)S(1)} %get-tuple-element.21), channel_id=1, source_target_pairs={{32,64},{64,32},{96,128},{128,96},{160,192},{192,160},{224,256},{2... | collective-permute-start | bytes 933896 | tf_op jit(solution)/shard_map/ppermute | solution.py:532
  15.0 1.9 %collective-permute-start.1 = (f32[38,16,128]{2,1,0:T(8,128)S(1)}, f32[38,16,128]{2,1,0:T(8,128)S(1)}, u32[]{:S(2)}, u32[]{:S(2)}) collective-permute-start(f32[38,16,128]{2,1,0:T(8,128)S(1)} %get-tuple-element.22), channel_id=1, source_target_pairs={{0,32},{32,0},{64,96},{96,64},{128,160},{160,128},{192,224},{224,1... | collective-permute-start | bytes 933896 | tf_op jit(solution)/shard_map/ppermute | solution.py:533
  16.9 0.0 copy-done
  16.9 0.0 copy-done.1
  16.9 0.8 %end_rows.1 = (f32[6,19,16,128]{3,2,1,0:T(8,128)S(1)}, bf16[288,384]{1,0:T(8,128)(2,1)S(1)}, bf16[144,384]{1,0:T(8,128)(2,1)S(1)}) custom-call(f32[19,256,128]{2,1,0:T(8,128)S(1)} %bitcast.4, s32[1,128]{1,0:T(1,128)S(1)} %bitcast.7), custom_call_target="tpu_custom_call" | custom-call | flops 5000000 | bytes 3500000 | tf_op jit(solution)/shard_map/end_rows/pallas_call | solution.py:534
  17.7 4.3 %collective-permute-done.xb = f32[38,16,128]{2,1,0:T(8,128)S(1)} collective-permute-done((f32[38,16,128]{2,1,0:T(8,128)S(1)}, f32[38,16,128]{2,1,0:T(8,128)S(1)}, u32[]{:S(2)}, u32[]{:S(2)}) %collective-permute-start) | collective-permute-done | bytes 311328 | tf_op jit(solution)/shard_map/ppermute | solution.py:532
  22.1 0.0 collective-permute-done.1.xa
  22.1 0.6 %y_pack.1 = (f32[324,128]{1,0:T(8,128)S(1)}, f32[328,128]{1,0:T(8,128)S(1)}, f32[6,19,40,128]{3,2,1,0:T(8,128)S(1)}) custom-call(f32[6,19,16,128]{3,2,1,0:T(8,128)S(1)} %get-tuple-element.20.g_ref, f32[38,16,128]{2,1,0:T(8,128)S(1)} %collective-permute-done.xb, f32[38,16,128]{2,1,0:T(8,128)S(1)} %collective-permute-done.1.xa), custom_call_target="tpu_custom_call" | custom-call | flops 5000000 | bytes 2000000 | tf_op jit(solution)/shard_map/y_pack/pallas_call | solution.py:547
  22.6 10.4 %collective-permute-start.2 = (f32[328,128]{1,0:T(8,128)S(1)}, f32[328,128]{1,0:T(8,128)S(1)}, u32[]{:S(2)}, u32[]{:S(2)}) collective-permute-start(f32[328,128]{1,0:T(8,128)S(1)} %get-tuple-element.23), channel_id=1, source_target_pairs={{1,2},{2,1},{3,4},{4,3},{5,6},{6,5},{7,8},{8,7},{9,10},{10,9},{11,... | collective-permute-start | bytes 503816 | tf_op jit(solution)/shard_map/ppermute | solution.py:561
  33.1 1.9 %collective-permute-start.3 = (f32[324,128]{1,0:T(8,128)S(1)}, f32[324,128]{1,0:T(8,128)S(1)}, u32[]{:S(2)}, u32[]{:S(2)}) collective-permute-start(f32[324,128]{1,0:T(8,128)S(1)} %get-tuple-element.29), channel_id=1, source_target_pairs={{0,1},{1,0},{2,3},{3,2},{4,5},{5,4},{6,7},{7,6},{8,9},{9,8},{10,11... | collective-permute-start | bytes 497672 | tf_op jit(solution)/shard_map/ppermute | solution.py:562
  35.0 5.3 %inside.1 = (f32[19,16,16,128]{3,2,1,0:T(8,128)S(1)}, f32[2,14,24,128]{3,2,1,0:T(8,128)S(1)}, f32[2,4,24,128]{3,2,1,0:T(8,128)S(1)}, f32[4,4,24,128]{3,2,1,0:T(8,128)S(1)}, f32[9,128]{1,0:T(8,128)S(1)}) custom-call(f32[19,256,128]{2,1,0:T(8,128)S(1)} %bitcast.5, f32[6,19,40,128]{3,2,1,0:T(8,128)S(1)} %get-tuple-element.24.t, ...), custom_call_target="tpu_custom_call" | custom-call | flops 50000000 | bytes 30000000 | tf_op jit(solution)/shard_map/inside/pallas_call | solution.py:563
  40.3 0.1 collective-permute-done.3.ya
  40.3 1.6 %first_side.1 = (f32[19,16,2,8,128]{4,3,2,1,0:T(8,128)}, f32[9,128]{1,0:T(8,128)S(1)}) custom-call(f32[324,128]{1,0:T(8,128)S(1)} %collective-permute-done.3.ya, f32[19,16,2,8,128]{4,3,2,1,0:T(8,128)S(1)} %bitcast.6, f32[2,14,24,128]{3,2,1,0:T(8,128)S(1)} %get-tuple-element.26.fw, f32[2,4,24,128]{3,2,1,0:T(8,128)S(1)} %get-tuple-element.27.qw, ...), custom_call_target="tpu_custom_call" | custom-call | flops 5000000 | bytes 4000000 | tf_op jit(solution)/shard_map/first_side/pallas_call | solution.py:591
  41.9 7.4 %collective-permute-done.2.yb = f32[328,128]{1,0:T(8,128)S(1)} collective-permute-done((f32[328,128]{1,0:T(8,128)S(1)}, f32[328,128]{1,0:T(8,128)S(1)}, u32[]{:S(2)}, u32[]{:S(2)}) %collective-permute-start.2) | collective-permute-done | bytes 167968 | tf_op jit(solution)/shard_map/ppermute | solution.py:561
  49.3 1.6 %second_side.1 = (f32[19,16,16,128]{3,2,1,0:T(8,128)}, f32[9,1,1,128]{3,2,1,0:T(1,128)}, f32[1,1,128]{2,1,0:T(1,128)}, f32[1,1,128]{2,1,0:T(1,128)}, f32[1,1,128]{2,1,0:T(1,128)}) custom-call(f32[328,128]{1,0:T(8,128)S(1)} %collective-permute-done.2.yb, f32[2,14,24,128]{3,2,1,0:T(8,128)S(1)} %get-tuple-element.26.fw, ...), custom_call_target="tpu_custom_call", output_to_operand_aliasing={{0}: (7, {})} | custom-call | flops 5000000 | bytes 3000000 | tf_op jit(solution)/shard_map/second_side/pallas_call | solution.py:601
Async XLA Ops:
  0.6 16.3 %copy-start = (f32[19,16,16,128]{3,2,1,0:T(8,128)S(1)}, f32[19,16,16,128]{3,2,1,0:T(8,128)}, u32[]{:S(2)}) copy-start(f32[19,16,16,128]{3,2,1,0:T(8,128)} %param.2) | copy-start | bytes 7471108
  0.6 16.3 %copy-start.1 = (s32[1,1,128]{2,1,0:T(1,128)S(1)}, s32[1,1,128]{2,1,0:T(1,128)}, u32[]{:S(2)}) copy-start(s32[1,1,128]{2,1,0:T(1,128)} %param.3) | copy-start | bytes 1540
  2.4 19.7 %collective-permute-start = (f32[38,16,128]{2,1,0:T(8,128)S(1)}, f32[38,16,128]{2,1,0:T(8,128)S(1)}, u32[]{:S(2)}, u32[]{:S(2)}) collective-permute-start(f32[38,16,128]{2,1,0:T(8,128)S(1)} %get-tuple-element.21), channel_id=1, source_target_pairs={{32,64},{64,32},{96,128},{128,96},{160,192},{192,160},{224,256},{2... | collective-permute-start | bytes 933896 | tf_op jit(solution)/shard_map/ppermute | solution.py:532
  15.0 7.1 %collective-permute-start.1 = (f32[38,16,128]{2,1,0:T(8,128)S(1)}, f32[38,16,128]{2,1,0:T(8,128)S(1)}, u32[]{:S(2)}, u32[]{:S(2)}) collective-permute-start(f32[38,16,128]{2,1,0:T(8,128)S(1)} %get-tuple-element.22), channel_id=1, source_target_pairs={{0,32},{32,0},{64,96},{96,64},{128,160},{160,128},{192,224},{224,1... | collective-permute-start | bytes 933896 | tf_op jit(solution)/shard_map/ppermute | solution.py:533
  22.6 26.7 %collective-permute-start.2 = (f32[328,128]{1,0:T(8,128)S(1)}, f32[328,128]{1,0:T(8,128)S(1)}, u32[]{:S(2)}, u32[]{:S(2)}) collective-permute-start(f32[328,128]{1,0:T(8,128)S(1)} %get-tuple-element.23), channel_id=1, source_target_pairs={{1,2},{2,1},{3,4},{4,3},{5,6},{6,5},{7,8},{8,7},{9,10},{10,9},{11,... | collective-permute-start | bytes 503816 | tf_op jit(solution)/shard_map/ppermute | solution.py:561
  33.1 7.3 %collective-permute-start.3 = (f32[324,128]{1,0:T(8,128)S(1)}, f32[324,128]{1,0:T(8,128)S(1)}, u32[]{:S(2)}, u32[]{:S(2)}) collective-permute-start(f32[324,128]{1,0:T(8,128)S(1)} %get-tuple-element.29), channel_id=1, source_target_pairs={{0,1},{1,0},{2,3},{3,2},{4,5},{5,4},{6,7},{7,6},{8,9},{9,8},{10,11... | collective-permute-start | bytes 497672 | tf_op jit(solution)/shard_map/ppermute | solution.py:562

commit v5 on v4

--- a/solution.py
+++ b/solution.py
@@ -44,10 +44,14 @@
 WIDE = 24
 YW = 20
 N_A = 5
-S_OFF = 13 * YW
-Y_LEN = S_OFF + 4 * N
+BW = 18
+B_OFF = N_A * YW
+P_OFF = B_OFF + N_A * BW
+S_OFF = P_OFF + 3 * YW
+E_OFF = S_OFF + 4 * N
+Y_LEN = E_OFF + 4
 PAD_LEN = 336
-FAR_LEN = 328
+FAR_LEN = 320
 V_ROWS = (-1, 0, 1, 14, 15, 16)
 UNROLL = 4
 VMEM_LIMIT = 28 * 1024 * 1024
@@ -217,8 +221,12 @@
             arrive[i] = KEEP * moved(rows[0], i, T_AT, N, 2)
         sums = moments(arrive, toward + par)
         parts = [(k * YW, v[:YW]) for k, v in enumerate(first)]
-        parts += [((N_A + k) * YW, beyond[i][:YW]) for k, i in enumerate(toward)]
-        parts += [((2 * N_A + k) * YW, v[:YW]) for k, v in enumerate((mom[0], mom[1], mom[3]))]
+        parts += [(B_OFF + k * BW, beyond[i][1 : 1 + BW]) for k, i in enumerate(toward)]
+        parts += [(P_OFF + k * YW, v[:YW]) for k, v in enumerate((mom[0], mom[1], mom[3]))]
+        for k, (at, inward) in enumerate(((0, 1), (YW - 1, -1))):
+            alone = [i for i in toward if C[i][0] == inward][0]
+            others = add_up(beyond[i] for i in toward if i != alone)
+            parts += [(E_OFF + 2 * k, beyond[alone][at : at + 1]), (E_OFF + 2 * k + 1, others[at : at + 1])]
         parts += [(S_OFF + k * N, v) for k, v in enumerate(sums)]
 
         def put(out, parts=parts):
@@ -354,7 +362,7 @@
         pick_out[pl.ds(k, 1)] = got[k]
 
 
-def side_cells(side, msg, fw, qw, pm, hs, hp, ep, store):
+def side_cells(side, msg, fw, qw, pm, hs, hp, ep, cb, store):
     row_x = lax.broadcasted_iota(jnp.int32, (WIDE, NZ), 0) - 2
     near = (row_x >= -1) & (row_x <= N)
     own = (row_x >= 0) & (row_x < N)
@@ -370,12 +378,21 @@
     out = collide(f)
     for i in ALL:
         hs[i, pl.ds(8, WIDE)] = out[i]
-    coming = {i: field(N_A + k) for k, i in enumerate(toward)}
+    cb[...] = jnp.zeros_like(cb)
+    for k in range(N_A):
+        cb[k, pl.ds(1, BW)] = msg[pl.ds(B_OFF + k * BW, BW)]
+    middle = [k for k, i in enumerate(toward) if C[i][0] == 0][0]
+    for k, (at, inward) in enumerate(((0, 1), (YW - 1, -1))):
+        alone = [k for k, i in enumerate(toward) if C[i][0] == inward][0]
+        cb[alone, pl.ds(at, 1)] = msg[pl.ds(E_OFF + 2 * k, 1)]
+        cb[middle, pl.ds(at, 1)] = msg[pl.ds(E_OFF + 2 * k + 1, 1)]
+    coming = {i: cb[k] for k, i in enumerate(toward)}
+    part = [msg[pl.ds(P_OFF + k * YW, WIDE)] for k in range(3)]
     mom = [
-        field(2 * N_A) + qw[side, 0],
-        field(2 * N_A + 1) + qw[side, 1],
+        part[0] + qw[side, 0],
+        part[1] + qw[side, 1],
         moment(coming, 1, toward) + qw[side, 2],
-        field(2 * N_A + 2) + qw[side, 3],
+        part[2] + qw[side, 3],
     ]
     eq = equil(mom, toward + par)
     for k, i in enumerate(toward):
@@ -420,7 +437,7 @@
     return picks(v, hot[pl.ds(3 * WIDE * side, 3 * WIDE)], zs)
 
 
-def first_side_kernel(ya, f_in, fw, qw, pm, pick, hot, seed_ref, out_hbm, pick_out, msg, hs, hp, ep, fs, sems):
+def first_side_kernel(ya, f_in, fw, qw, pm, pick, hot, seed_ref, out_hbm, pick_out, msg, hs, hp, ep, cb, fs, sems):
     msg[pl.ds(0, Y_LEN)] = ya[...]
 
     def work(side):
@@ -432,7 +449,7 @@
             for i in ALL:
                 copies.append(half_out(i, side, f_in, fs, out_hbm, sems, patches.get(i, [])))
 
-        vel = side_cells(side, msg, fw, qw, pm, hs, hp, ep, store)
+        vel = side_cells(side, msg, fw, qw, pm, hs, hp, ep, cb, store)
         zs = lax.rem(seed_ref[...], NZ)
         got = side_picks(side, vel, hot, zs)
         for k in range(9):
@@ -446,7 +463,7 @@
 
 
 def second_side_kernel(
-    yb, fw, qw, pm, pick, hot, seed_ref, _, out_hbm, grad_out, q_out, r_out, s_out, msg, hs, hp, ep, rows, sems
+    yb, fw, qw, pm, pick, hot, seed_ref, _, out_hbm, grad_out, q_out, r_out, s_out, msg, hs, hp, ep, cb, rows, sems
 ):
     msg[pl.ds(0, FAR_LEN)] = yb[...]
 
@@ -461,7 +478,7 @@
                     copies.append(pltpu.make_async_copy(rows.at[k], out_hbm.at[i, :, y], sems.at[k]))
                     copies[k].start()
 
-        vel = side_cells(side, msg, fw, qw, pm, hs, hp, ep, store)
+        vel = side_cells(side, msg, fw, qw, pm, hs, hp, ep, cb, store)
         zs = lax.rem(seed_ref[...], NZ)
         got = side_picks(side, vel, hot, zs)
         comps = [(got[k] + pick[pl.ds(k, 1)]) * SCALE for k in range(9)]
@@ -587,6 +604,7 @@
         vmem((19, T_LEN, NZ), F32),
         vmem((N_A, T_LEN, NZ), F32),
         vmem((9, T_LEN, NZ), F32),
+        vmem((N_A, WIDE, NZ), F32),
     ]
     half, pick = pl.pallas_call(
         first_side_kernel,

time: 51.2 us -> 50.8 us (level)
  transfers between devices with their start and end apart: 4 -> 4, of which waited for: 3 -> 2; matrix products, arithmetic and copies ran while one was open for 0% -> 0% of each run, Pallas kernels for 15% -> 15%
where the time goes in v5:
time: 50.8 us; the launch traced here: 50.6 us
  starting transfers between devices  26.9 us (53%)
  waiting for transfers between devices  11.4 us (22%)
  Pallas kernels  10.2 us (20%)
  local copies, waits for them, and re-layouts  1.39 us (3%)
  between operations  0.74 us (1%)
    ppermute x1, starting transfers between devices, per_device(): xb = lax.ppermute(xb, 'gx', x_second)  12.6 us
    ppermute x1, starting transfers between devices, per_device(): yb = lax.ppermute(yb, 'gy', y_second)  10.4 us
    ppermute x1, waiting for transfers between devices, per_device(): yb = lax.ppermute(yb, 'gy', y_second)  7.07 us
    pallas_call x1, Pallas kernels, per_device(): pl.pallas_call(inside_kernel, out_shape=[shape(19, N, N, NZ), shape(2, 14...  5.26 us
    ppermute x1, waiting for transfers between devices, per_device(): xb = lax.ppermute(xb, 'gx', x_second)  4.32 us
    ppermute x1, starting transfers between devices, per_device(): xa = lax.ppermute(xa, 'gx', x_first)  1.92 us
    ppermute x1, starting transfers between devices, per_device(): ya = lax.ppermute(ya, 'gy', y_first)  1.92 us
    pallas_call x1, Pallas kernels, per_device(): pl.pallas_call(second_side_kernel, out_shape=[shape(19, N, N, NZ), shape(...  1.63 us
  transfers between devices with their start and end apart: 4, of which 2 were waited for; matrix products, arithmetic and copies ran while one was open for 0% of the time, Pallas kernels for 15%

profile of v5, /device:TPU:30, one launch (start us, length us, event | category | flops | bytes accessed | tf_op | source)
XLA Modules:
  0.0 50.6 jit_solution(14311126779255120061)
XLA Ops:
  0.6 0.0 copy-start
  0.6 0.0 copy-start.1
  0.7 1.4 %fusion = (f32[19,3,16,128]{3,2,1,0:T(8,128)S(1)}, f32[19,3,16,128]{3,2,1,0:T(8,128)S(1)}) fusion(f32[19,16,16,128]{3,2,1,0:T(8,128)} %param.2), kind=kLoop, calls=%fused_computation | loop fusion | bytes 1867776 | tf_op jit(solution)/shard_map/slice | solution.py:548
  2.0 0.3 x_pack.1
  2.4 12.6 %collective-permute-start = (f32[38,16,128]{2,1,0:T(8,128)S(1)}, f32[38,16,128]{2,1,0:T(8,128)S(1)}, u32[]{:S(2)}, u32[]{:S(2)}) collective-permute-start(f32[38,16,128]{2,1,0:T(8,128)S(1)} %get-tuple-element.21), channel_id=1, source_target_pairs={{32,64},{64,32},{96,128},{128,96},{160,192},{192,160},{224,256},{2... | collective-permute-start | bytes 933896 | tf_op jit(solution)/shard_map/ppermute | solution.py:549
  15.0 1.9 %collective-permute-start.1 = (f32[38,16,128]{2,1,0:T(8,128)S(1)}, f32[38,16,128]{2,1,0:T(8,128)S(1)}, u32[]{:S(2)}, u32[]{:S(2)}) collective-permute-start(f32[38,16,128]{2,1,0:T(8,128)S(1)} %get-tuple-element.22), channel_id=1, source_target_pairs={{0,32},{32,0},{64,96},{96,64},{128,160},{160,128},{192,224},{224,1... | collective-permute-start | bytes 933896 | tf_op jit(solution)/shard_map/ppermute | solution.py:550
  16.9 0.0 copy-done
  16.9 0.0 copy-done.1
  16.9 0.8 %end_rows.1 = (f32[6,19,16,128]{3,2,1,0:T(8,128)S(1)}, bf16[288,384]{1,0:T(8,128)(2,1)S(1)}, bf16[144,384]{1,0:T(8,128)(2,1)S(1)}) custom-call(f32[19,256,128]{2,1,0:T(8,128)S(1)} %bitcast.4, s32[1,128]{1,0:T(1,128)S(1)} %bitcast.7), custom_call_target="tpu_custom_call" | custom-call | flops 5000000 | bytes 3500000 | tf_op jit(solution)/shard_map/end_rows/pallas_call | solution.py:551
  17.7 4.3 %collective-permute-done.xb = f32[38,16,128]{2,1,0:T(8,128)S(1)} collective-permute-done((f32[38,16,128]{2,1,0:T(8,128)S(1)}, f32[38,16,128]{2,1,0:T(8,128)S(1)}, u32[]{:S(2)}, u32[]{:S(2)}) %collective-permute-start) | collective-permute-done | bytes 311328 | tf_op jit(solution)/shard_map/ppermute | solution.py:549
  22.1 0.0 collective-permute-done.1.xa
  22.1 0.6 %y_pack.1 = (f32[318,128]{1,0:T(8,128)S(1)}, f32[320,128]{1,0:T(8,128)S(1)}, f32[6,19,40,128]{3,2,1,0:T(8,128)S(1)}) custom-call(f32[6,19,16,128]{3,2,1,0:T(8,128)S(1)} %get-tuple-element.20.g_ref, f32[38,16,128]{2,1,0:T(8,128)S(1)} %collective-permute-done.xb, f32[38,16,128]{2,1,0:T(8,128)S(1)} %collective-permute-done.1.xa), custom_call_target="tpu_custom_call" | custom-call | flops 5000000 | bytes 2000000 | tf_op jit(solution)/shard_map/y_pack/pallas_call | solution.py:564
  22.6 10.4 %collective-permute-start.2 = (f32[320,128]{1,0:T(8,128)S(1)}, f32[320,128]{1,0:T(8,128)S(1)}, u32[]{:S(2)}, u32[]{:S(2)}) collective-permute-start(f32[320,128]{1,0:T(8,128)S(1)} %get-tuple-element.23), channel_id=1, source_target_pairs={{1,2},{2,1},{3,4},{4,3},{5,6},{6,5},{7,8},{8,7},{9,10},{10,9},{11,... | collective-permute-start | bytes 491528 | tf_op jit(solution)/shard_map/ppermute | solution.py:578
  33.1 1.9 %collective-permute-start.3 = (f32[318,128]{1,0:T(8,128)S(1)}, f32[318,128]{1,0:T(8,128)S(1)}, u32[]{:S(2)}, u32[]{:S(2)}) collective-permute-start(f32[318,128]{1,0:T(8,128)S(1)} %get-tuple-element.29), channel_id=1, source_target_pairs={{0,1},{1,0},{2,3},{3,2},{4,5},{5,4},{6,7},{7,6},{8,9},{9,8},{10,11... | collective-permute-start | bytes 488456 | tf_op jit(solution)/shard_map/ppermute | solution.py:579
  35.0 5.3 %inside.1 = (f32[19,16,16,128]{3,2,1,0:T(8,128)S(1)}, f32[2,14,24,128]{3,2,1,0:T(8,128)S(1)}, f32[2,4,24,128]{3,2,1,0:T(8,128)S(1)}, f32[4,4,24,128]{3,2,1,0:T(8,128)S(1)}, f32[9,128]{1,0:T(8,128)S(1)}) custom-call(f32[19,256,128]{2,1,0:T(8,128)S(1)} %bitcast.5, f32[6,19,40,128]{3,2,1,0:T(8,128)S(1)} %get-tuple-element.24.t, ...), custom_call_target="tpu_custom_call" | custom-call | flops 50000000 | bytes 30000000 | tf_op jit(solution)/shard_map/inside/pallas_call | solution.py:580
  40.3 0.0 collective-permute-done.3.ya
  40.3 1.6 %first_side.1 = (f32[19,16,2,8,128]{4,3,2,1,0:T(8,128)}, f32[9,128]{1,0:T(8,128)S(1)}) custom-call(f32[318,128]{1,0:T(8,128)S(1)} %collective-permute-done.3.ya, f32[19,16,2,8,128]{4,3,2,1,0:T(8,128)S(1)} %bitcast.6, f32[2,14,24,128]{3,2,1,0:T(8,128)S(1)} %get-tuple-element.26.fw, f32[2,4,24,128]{3,2,1,0:T(8,128)S(1)} %get-tuple-element.27.qw, ...), custom_call_target="tpu_custom_call" | custom-call | flops 5000000 | bytes 4000000 | tf_op jit(solution)/shard_map/first_side/pallas_call | solution.py:609
  41.9 7.1 %collective-permute-done.2.yb = f32[320,128]{1,0:T(8,128)S(1)} collective-permute-done((f32[320,128]{1,0:T(8,128)S(1)}, f32[320,128]{1,0:T(8,128)S(1)}, u32[]{:S(2)}, u32[]{:S(2)}) %collective-permute-start.2) | collective-permute-done | bytes 163872 | tf_op jit(solution)/shard_map/ppermute | solution.py:578
  49.0 1.6 %second_side.1 = (f32[19,16,16,128]{3,2,1,0:T(8,128)}, f32[9,1,1,128]{3,2,1,0:T(1,128)}, f32[1,1,128]{2,1,0:T(1,128)}, f32[1,1,128]{2,1,0:T(1,128)}, f32[1,1,128]{2,1,0:T(1,128)}) custom-call(f32[320,128]{1,0:T(8,128)S(1)} %collective-permute-done.2.yb, f32[2,14,24,128]{3,2,1,0:T(8,128)S(1)} %get-tuple-element.26.fw, ...), custom_call_target="tpu_custom_call", output_to_operand_aliasing={{0}: (7, {})} | custom-call | flops 5000000 | bytes 3000000 | tf_op jit(solution)/shard_map/second_side/pallas_call | solution.py:619
Async XLA Ops:
  0.6 16.3 %copy-start = (f32[19,16,16,128]{3,2,1,0:T(8,128)S(1)}, f32[19,16,16,128]{3,2,1,0:T(8,128)}, u32[]{:S(2)}) copy-start(f32[19,16,16,128]{3,2,1,0:T(8,128)} %param.2) | copy-start | bytes 7471108
  0.6 16.3 %copy-start.1 = (s32[1,1,128]{2,1,0:T(1,128)S(1)}, s32[1,1,128]{2,1,0:T(1,128)}, u32[]{:S(2)}) copy-start(s32[1,1,128]{2,1,0:T(1,128)} %param.3) | copy-start | bytes 1540
  2.4 19.7 %collective-permute-start = (f32[38,16,128]{2,1,0:T(8,128)S(1)}, f32[38,16,128]{2,1,0:T(8,128)S(1)}, u32[]{:S(2)}, u32[]{:S(2)}) collective-permute-start(f32[38,16,128]{2,1,0:T(8,128)S(1)} %get-tuple-element.21), channel_id=1, source_target_pairs={{32,64},{64,32},{96,128},{128,96},{160,192},{192,160},{224,256},{2... | collective-permute-start | bytes 933896 | tf_op jit(solution)/shard_map/ppermute | solution.py:549
  15.0 7.1 %collective-permute-start.1 = (f32[38,16,128]{2,1,0:T(8,128)S(1)}, f32[38,16,128]{2,1,0:T(8,128)S(1)}, u32[]{:S(2)}, u32[]{:S(2)}) collective-permute-start(f32[38,16,128]{2,1,0:T(8,128)S(1)} %get-tuple-element.22), channel_id=1, source_target_pairs={{0,32},{32,0},{64,96},{96,64},{128,160},{160,128},{192,224},{224,1... | collective-permute-start | bytes 933896 | tf_op jit(solution)/shard_map/ppermute | solution.py:550
  22.6 26.4 %collective-permute-start.2 = (f32[320,128]{1,0:T(8,128)S(1)}, f32[320,128]{1,0:T(8,128)S(1)}, u32[]{:S(2)}, u32[]{:S(2)}) collective-permute-start(f32[320,128]{1,0:T(8,128)S(1)} %get-tuple-element.23), channel_id=1, source_target_pairs={{1,2},{2,1},{3,4},{4,3},{5,6},{6,5},{7,8},{8,7},{9,10},{10,9},{11,... | collective-permute-start | bytes 491528 | tf_op jit(solution)/shard_map/ppermute | solution.py:578
  33.1 7.2 %collective-permute-start.3 = (f32[318,128]{1,0:T(8,128)S(1)}, f32[318,128]{1,0:T(8,128)S(1)}, u32[]{:S(2)}, u32[]{:S(2)}) collective-permute-start(f32[318,128]{1,0:T(8,128)S(1)} %get-tuple-element.29), channel_id=1, source_target_pairs={{0,1},{1,0},{2,3},{3,2},{4,5},{5,4},{6,7},{7,6},{8,9},{9,8},{10,11... | collective-permute-start | bytes 488456 | tf_op jit(solution)/shard_map/ppermute | solution.py:579
